TPU v7x, 512 devices: a whole 4x8x8 slice. The times are simulated.
512 devices in a mesh: dp: 64 (over y, x, core), mp: 8 (over z).
Axes of the slice: x: 4, y: 8, z: 8, core: 2. Of those that a mesh axis runs over, the one named last changes fastest.
Arguments:
- partial_grads: bfloat16 [64, 2, 2, 512, 4096], P('dp', None, None, None, 'mp')
- factors: bfloat16 [8, 8, 512, 1024], P('mp', None, 'dp'), as said below
- inverse_factors: bfloat16 [8, 8, 512, 1024], P('mp', None, 'dp'), as said below
- probes: bfloat16 [8, 8, 512, 512], P('mp', None, 'dp'), may hold values from -6 to 6
- slot_table: int32 [8, 4], P('mp'), may hold values from 0 to 7, as said below
Outputs:
- preconditioned: bfloat16 [2, 2, 512, 4096], P(None, None, 'dp', 'mp')
- new_factors: bfloat16 [8, 8, 512, 1024], P('mp', None, 'dp')
Inputs may be any that keep to these rules, and one draw needn't show every extreme that they name: `slot_table`: in each row the 4 entries are distinct slots; slot j belongs to owner j // 2 (an owner is a group of 16 consecutive dp devices; the starting program sends slots 2k and 2k+1 to dp device 16k for updating), and in every row some owner holds 2 blocks. `factors`: both halves of every slot are upper triangular with a positive diagonal. `inverse_factors`: both halves of every slot are upper triangular with a positive diagonal.
All inputs are finite; a program needn't handle non-finite values. Where the computation divides by a largest or mean magnitude, that divisor is 1e-20 or more.
Results may differ from a plain program's by a relative error of at most 0.011.
Values may be sent and summed in bfloat16 or wider, within the bound.
A program may use at most 64 MiB of HBM per device.

v0:
```python
import math

import jax
import jax.numpy as jnp
import numpy as np
from jax import lax
from jax.sharding import PartitionSpec as P

GROUP = 16


CLIP_RMS = 0.3
LEARN_RATE = 0.1
EPS_NORM = 1e-06


def product(left_op, right_op):
    return jnp.dot(left_op, right_op, preferred_element_type=jnp.float32)


def step_factor(factor, first_gram, second_gram):
    bound_value = jnp.max(jnp.abs(first_gram + second_gram)) + EPS_NORM
    change = jnp.triu(first_gram - second_gram).astype(jnp.bfloat16)
    moved_rows = product(change, factor)
    return (factor.astype(jnp.float32) - LEARN_RATE / bound_value * moved_rows).astype(jnp.bfloat16)


def update_block(gradient, left_q, right_q, left_inv, right_inv, probe_mat):
    left_times = product(left_q, gradient).astype(jnp.bfloat16)
    whitened = product(left_times, right_q.T).astype(jnp.bfloat16)
    half_conjugate = product(left_inv.T, probe_mat).astype(jnp.bfloat16)
    conjugate = product(half_conjugate, right_inv).astype(jnp.bfloat16)
    new_left = step_factor(left_q, product(whitened, whitened.T), product(conjugate, conjugate.T))
    new_right = step_factor(right_q, product(whitened.T, whitened), product(conjugate.T, conjugate))
    precond_left = product(new_left.T, new_left).astype(jnp.bfloat16)
    precond_right = product(new_right.T, new_right).astype(jnp.bfloat16)
    middle = product(precond_left, gradient).astype(jnp.bfloat16)
    result = product(middle, precond_right).astype(jnp.bfloat16)
    return (result, jnp.concatenate([new_left, new_right], axis=1))


def pick_slots(onehot, source):
    return jnp.einsum("bj,jrc->brc", onehot, source, preferred_element_type=jnp.float32).astype(
        jnp.bfloat16
    )


def place_slots(onehot, source):
    return jnp.einsum("bj,brc->jrc", onehot, source, preferred_element_type=jnp.float32).astype(
        jnp.bfloat16
    )


def body(partial_grads, factors, inverse_factors, probes, slot_table):
    devices = lax.axis_size("dp")
    my_index = lax.axis_index("dp")
    local_sum = partial_grads[0].astype(jnp.float32)
    experts, block_rows, block_size, columns = local_sum.shape
    summed = lax.psum_scatter(local_sum, "dp", scatter_dimension=2, tiled=True)
    rows_dev = summed.shape[2]
    blocks_col = experts * block_rows
    gradient = summed.reshape(blocks_col, rows_dev, columns)
    entry_count = blocks_col * block_size * columns * lax.axis_size("mp")
    squares = lax.psum(jnp.sum(gradient * gradient), ("dp", "mp"))
    clip_factor = jnp.minimum(1.0, CLIP_RMS * math.sqrt(entry_count) / jnp.sqrt(squares + EPS_NORM))
    clipped = (gradient * clip_factor).astype(jnp.bfloat16)
    old_state = factors[0]
    combined_state = jnp.concatenate([old_state, inverse_factors[0]], axis=2)
    probe_rows = probes[0]
    own_slots = old_state.shape[0]
    slot_row = slot_table[0]
    onehot = (slot_row[:, None] == jnp.arange(own_slots, dtype=jnp.int32)[None, :]).astype(
        jnp.bfloat16
    )
    occupied = jnp.sum(onehot.astype(jnp.float32), axis=0) > 0.5
    slots_dev = own_slots // (devices // GROUP)
    target = np.arange(own_slots) // slots_dev * GROUP
    position = np.arange(own_slots) % slots_dev
    unit_grad = place_slots(onehot, clipped)
    global_rows = my_index * rows_dev + jnp.arange(rows_dev, dtype=jnp.int32)
    diagonal = (jnp.arange(columns, dtype=jnp.int32)[None, :] == global_rows[:, None]).astype(
        jnp.bfloat16
    )
    filler = jnp.concatenate([diagonal, diagonal, diagonal, diagonal], axis=1)
    send_grad = (
        jnp.zeros((devices, slots_dev, rows_dev, columns), jnp.bfloat16)
        .at[target, position]
        .set(unit_grad)
    )
    send_state = (
        jnp.broadcast_to(filler, (devices, slots_dev, rows_dev, 4 * columns))
        .at[target, position]
        .set(combined_state)
    )
    send_probe = (
        jnp.zeros((devices, slots_dev, rows_dev, columns), jnp.bfloat16)
        .at[target, position]
        .set(probe_rows)
    )
    grad_in = lax.all_to_all(send_grad, "dp", split_axis=0, concat_axis=2, tiled=True)
    state_in = lax.all_to_all(send_state, "dp", split_axis=0, concat_axis=2, tiled=True)
    probe_in = lax.all_to_all(send_probe, "dp", split_axis=0, concat_axis=2, tiled=True)

    def run_one(item_set):
        state = item_set[1]
        return update_block(
            item_set[0],
            state[:, :block_size],
            state[:, block_size : 2 * block_size],
            state[:, 2 * block_size : 3 * block_size],
            state[:, 3 * block_size :],
            item_set[2],
        )

    result, moved_rows = lax.map(run_one, (grad_in[0], state_in[0], probe_in[0]))
    back_grad = lax.all_to_all(result[None], "dp", split_axis=2, concat_axis=0, tiled=True)
    back_state = lax.all_to_all(moved_rows[None], "dp", split_axis=2, concat_axis=0, tiled=True)
    unit_back = back_grad[target, position]
    state_back = back_state[target, position]
    precond = pick_slots(onehot, unit_back)
    new_state = jnp.where(occupied[:, None, None], state_back, old_state)
    return (precond.reshape(experts, block_rows, rows_dev, columns), new_state[None])


def solution(mesh):
    return jax.shard_map(
        body,
        mesh=mesh,
        in_specs=(
            P("dp", None, None, None, "mp"),
            P("mp", None, "dp", None),
            P("mp", None, "dp", None),
            P("mp", None, "dp", None),
            P("mp", None),
        ),
        out_specs=(P(None, None, "dp", "mp"), P("mp", None, "dp", None)),
        check_vma=False,
    )
```

profile of v0, /device:TPU:1, one launch (start us, length us, event | category | flops | bytes accessed | tf_op | source)
XLA Modules:
  0.0 513.3 jit_solution(15969105971914788014)
XLA Ops:
  8.3 2.3 scatter_fusion.2
  10.6 11.6 %all-to-all-start.2 = ((bf16[64,2,8,512]{3,2,1,0:T(8,128)(2,1)}), bf16[64,2,8,512]{3,2,1,0:T(8,128)(2,1)S(1)}, u32[]{:S(2)}, u32[]{:S(2)}) async-start(bf16[64,2,8,512]{3,2,1,0:T(8,128)(2,1)} %scatter_fusion.2), calls=%async_computation.3 | async-start | bytes 2097152 | tf_op jit(solution)/shard_map/all_to_all | solution.py:102
  22.4 2.5 broadcast_in_dim.73
  24.8 2.3 scatter_fusion
  27.1 23.1 %all-to-all-done.2 = bf16[64,2,8,512]{3,2,1,0:T(8,128)(2,1)S(1)} async-done(((bf16[64,2,8,512]{3,2,1,0:T(8,128)(2,1)}), bf16[64,2,8,512]{3,2,1,0:T(8,128)(2,1)S(1)}, u32[]{:S(2)}, u32[]{:S(2)}) %all-to-all-start.2) | async-done | bytes 1048608 | tf_op jit(solution)/shard_map/all_to_all | solution.py:102
  50.2 6.7 %all-to-all-start = ((bf16[64,2,8,2048]{3,2,1,0:T(8,128)(2,1)}), bf16[64,2,8,2048]{3,2,1,0:T(8,128)(2,1)}, u32[]{:S(2)}, u32[]{:S(2)}) async-start(bf16[64,2,8,2048]{3,2,1,0:T(8,128)(2,1)} %scatter_fusion), calls=%async_computation | async-start | bytes 8388608 | tf_op jit(solution)/shard_map/all_to_all | solution.py:101
  56.9 2.5 bitcast_convert_fusion
  59.5 153.9 %reduce-scatter.2.cloned.1.call-done = f32[2,2,8,512]{3,2,1,0:T(8,128)} async-done(((f32[2,2,512,512]{3,2,1,0:T(8,128)}), f32[2,2,8,512]{3,2,1,0:T(8,128)}) %reduce-scatter.2.cloned.1.call-update) | async-done | bytes 65552 | tf_op jit(solution)/shard_map/reduce_scatter | solution.py:59
  214.8 101.8 %psum.7 = f32[]{:T(128)} all-reduce(f32[]{:T(128)} %multiply_reduce_fusion), channel_id=1, replica_groups=mesh['dp'=64,'mp'=8] {'dp','mp'}, use_global_device_ids=true, to_apply=%region_2.0 | all-reduce | flops 1 | bytes 8 | tf_op jit(solution)/shard_map/psum | solution.py:64
  319.6 2.0 scatter_fusion.1
  321.6 8.7 %all-to-all-start.1 = ((bf16[64,2,8,512]{3,2,1,0:T(8,128)(2,1)}), bf16[64,2,8,512]{3,2,1,0:T(8,128)(2,1)S(1)}, u32[]{:S(2)}, u32[]{:S(2)}) async-start(bf16[64,2,8,512]{3,2,1,0:T(8,128)(2,1)} %scatter_fusion.1), calls=%async_computation.2 | async-start | bytes 2097152 | tf_op jit(solution)/shard_map/all_to_all | solution.py:100
  330.4 4.7 copy_bitcast_fusion
  335.1 23.2 %all-to-all-done.1 = bf16[64,2,8,512]{3,2,1,0:T(8,128)(2,1)S(1)} async-done(((bf16[64,2,8,512]{3,2,1,0:T(8,128)(2,1)}), bf16[64,2,8,512]{3,2,1,0:T(8,128)(2,1)S(1)}, u32[]{:S(2)}, u32[]{:S(2)}) %all-to-all-start.1) | async-done | bytes 1048608 | tf_op jit(solution)/shard_map/all_to_all | solution.py:100
  359.4 48.4 %while.12 = (s32[]{:T(128)}, bf16[2,512,512]{2,1,0:T(8,128)(2,1)}, bf16[2,512,1024]{1,2,0:T(8,128)(2,1)}, bf16[2,512,2048]{2,1,0:T(8,128)(2,1)}, bf16[2,512,512]...) while((s32[]{:T(128)}, bf16[2,512,512]{2,1,0:T(8,128)(2,1)}, ...), condition=%wide.region_9.10_spmd, body=%wide.region_6.9_spmd.sunk | while | flops 3768058368 | bytes 53485872 | solution.py:115
  359.4 2.1 constant_dynamic-slice_fusion.2
  361.5 2.5 copy.74
  367.1 1.9 convolution_convert_fusion.14
  370.9 2.6 fusion.115
  380.8 2.8 fusion.116
  383.5 2.1 constant_dynamic-slice_fusion.2
  385.6 2.5 copy.74
  391.3 1.9 convolution_convert_fusion.14
  395.1 2.6 fusion.115
  405.0 2.7 fusion.116
  407.7 3.3 copy.72
  411.0 6.5 %all-to-all-start.3 = ((bf16[1,2,512,512]{3,1,0,2:T(2,128)(2,1)}), bf16[1,2,512,512]{3,1,0,2:T(2,128)(2,1)S(1)}, u32[]{:S(2)}, u32[]{:S(2)}) async-start(bf16[1,2,512,512]{3,1,0,2:T(2,128)(2,1)} %bitcast.83), calls=%async_computation.4 | async-start | bytes 2097152 | tf_op jit(solution)/shard_map/all_to_all | solution.py:116
  417.5 6.3 %copy.50 = bf16[2,512,1024]{2,0,1:T(2,128)(2,1)} copy(bf16[2,512,1024]{1,2,0:T(8,128)(2,1)} %get-tuple-element.36) | data formatting | bytes 4194304 | tf_op jit(solution)/shard_map/while | solution.py:115
  423.8 21.7 %all-to-all-done.3 = bf16[1,2,512,512]{3,1,0,2:T(2,128)(2,1)S(1)} async-done(((bf16[1,2,512,512]{3,1,0,2:T(2,128)(2,1)}), bf16[1,2,512,512]{3,1,0,2:T(2,128)(2,1)S(1)}, u32[]{:S(2)}, u32[]{:S(2)}) %all-to-all-start.3) | async-done | bytes 1048608 | tf_op jit(solution)/shard_map/all_to_all | solution.py:116
  445.5 6.5 %all-to-all-start.4 = ((bf16[1,2,512,1024]{3,1,0,2:T(2,128)(2,1)}), bf16[1,2,512,1024]{3,1,0,2:T(2,128)(2,1)S(1)}, u32[]{:S(2)}, u32[]{:S(2)}) async-start(bf16[1,2,512,1024]{3,1,0,2:T(2,128)(2,1)} %bitcast.26), calls=%async_computation.5 | async-start | bytes 4194304 | tf_op jit(solution)/shard_map/all_to_all | solution.py:117
  455.9 45.7 %all-to-all-done.4 = bf16[1,2,512,1024]{3,1,0,2:T(2,128)(2,1)S(1)} async-done(((bf16[1,2,512,1024]{3,1,0,2:T(2,128)(2,1)}), bf16[1,2,512,1024]{3,1,0,2:T(2,128)(2,1)S(1)}, u32[]{:S(2)}, u32[]{:S(2)}) %all-to-all-start.4) | async-done | bytes 2097184 | tf_op jit(solution)/shard_map/all_to_all | solution.py:117
  501.6 1.9 copy.70
  503.6 2.2 gather_fusion.1
  (72 shorter events, 32.4 us)
Async XLA Ops:
  7.2 15.1 %copy-start.7 = (bf16[1,8,8,1024]{3,2,1,0:T(8,128)(2,1)S(1)}, bf16[1,8,8,1024]{3,2,1,0:T(8,128)(2,1)}, u32[]{:S(2)}) copy-start(bf16[1,8,8,1024]{3,2,1,0:T(8,128)(2,1)} %param.20) | copy-start | bytes 393220
  7.2 15.1 %copy-start.8 = (bf16[1,8,8,1024]{3,2,1,0:T(8,128)(2,1)S(1)}, bf16[1,8,8,1024]{3,2,1,0:T(8,128)(2,1)}, u32[]{:S(2)}) copy-start(bf16[1,8,8,1024]{3,2,1,0:T(8,128)(2,1)} %param.21) | copy-start | bytes 393220
  10.6 39.6 %all-to-all-start.2 = ((bf16[64,2,8,512]{3,2,1,0:T(8,128)(2,1)}), bf16[64,2,8,512]{3,2,1,0:T(8,128)(2,1)S(1)}, u32[]{:S(2)}, u32[]{:S(2)}) async-start(bf16[64,2,8,512]{3,2,1,0:T(8,128)(2,1)} %scatter_fusion.2), calls=%async_computation.3 | async-start | bytes 2097152 | tf_op jit(solution)/shard_map/all_to_all | solution.py:102
  22.3 2.5 copy-start.6
  27.1 29.8 %copy-start.1 = (bf16[1,2,2,512,512]{4,3,2,1,0:T(8,128)(2,1)S(1)}, bf16[1,2,2,512,512]{4,3,2,1,0:T(8,128)(2,1)}, u32[]{:S(2)}) copy-start(bf16[1,2,2,512,512]{4,3,2,1,0:T(8,128)(2,1)} %param.19) | copy-start | bytes 6291460
  50.2 271.4 %all-to-all-start = ((bf16[64,2,8,2048]{3,2,1,0:T(8,128)(2,1)}), bf16[64,2,8,2048]{3,2,1,0:T(8,128)(2,1)}, u32[]{:S(2)}, u32[]{:S(2)}) async-start(bf16[64,2,8,2048]{3,2,1,0:T(8,128)(2,1)} %scatter_fusion), calls=%async_computation | async-start | bytes 8388608 | tf_op jit(solution)/shard_map/all_to_all | solution.py:101
  56.8 156.5 %reduce-scatter.2.cloned.1.call-start = ((), (), s32[]{:S(2)}) async-start(), calls=%async_computation.6 | async-start | bytes 4259840 | tf_op jit(solution)/shard_map/reduce_scatter | solution.py:59
  59.5 258.7 %copy-start.9 = (s32[1,4]{1,0:T(1,128)S(1)}, s32[1,4]{1,0:T(1,128)}, u32[]{:S(2)}) copy-start(s32[1,4]{1,0:T(1,128)} %param.23) | copy-start | bytes 52
  321.6 36.7 %all-to-all-start.1 = ((bf16[64,2,8,512]{3,2,1,0:T(8,128)(2,1)}), bf16[64,2,8,512]{3,2,1,0:T(8,128)(2,1)S(1)}, u32[]{:S(2)}, u32[]{:S(2)}) async-start(bf16[64,2,8,512]{3,2,1,0:T(8,128)(2,1)} %scatter_fusion.1), calls=%async_computation.2 | async-start | bytes 2097152 | tf_op jit(solution)/shard_map/all_to_all | solution.py:100
  359.4 4.6 copy-start.2
  365.9 1.2 copy-start.4
  375.1 2.6 copy-start
  377.6 1.6 copy-start.5
  380.8 2.8 copy-start.3
  383.5 4.6 copy-start.2
  390.1 1.2 copy-start.4
  399.3 2.6 copy-start
  401.8 1.6 copy-start.5
  405.0 2.7 copy-start.3
  411.0 34.5 %all-to-all-start.3 = ((bf16[1,2,512,512]{3,1,0,2:T(2,128)(2,1)}), bf16[1,2,512,512]{3,1,0,2:T(2,128)(2,1)S(1)}, u32[]{:S(2)}, u32[]{:S(2)}) async-start(bf16[1,2,512,512]{3,1,0,2:T(2,128)(2,1)} %bitcast.83), calls=%async_computation.4 | async-start | bytes 2097152 | tf_op jit(solution)/shard_map/all_to_all | solution.py:116
  445.5 56.1 %all-to-all-start.4 = ((bf16[1,2,512,1024]{3,1,0,2:T(2,128)(2,1)}), bf16[1,2,512,1024]{3,1,0,2:T(2,128)(2,1)S(1)}, u32[]{:S(2)}, u32[]{:S(2)}) async-start(bf16[1,2,512,1024]{3,1,0,2:T(2,128)(2,1)} %bitcast.26), calls=%async_computation.5 | async-start | bytes 4194304 | tf_op jit(solution)/shard_map/all_to_all | solution.py:117
Sparse Core Ops, SparseCore 0:
  62.4 150.9 reduce-scatter.1
where the time goes:
time: 516 us; the launch traced here: 513 us
  waiting for transfers between devices  268 us (52%)
  blocking collectives  102 us (20%)
  local copies, waits for them, and re-layouts  46.2 us (9%)
  starting transfers between devices  39.9 us (8%)
  matrix products  31.9 us (6%)
  between operations  14.9 us (3%)
  other arithmetic  7.96 us (2%)
    reduce_scatter x1, waiting for transfers between devices, body(): summed = lax.psum_scatter(local_sum, 'dp', scatter_dimension=2, tiled=True)  154 us
    psum x1, blocking collectives, body(): squares = lax.psum(jnp.sum(gradient * gradient), ('dp', 'mp'))  102 us
    all_to_all x1, waiting for transfers between devices, body(): lax.all_to_all(moved_rows[None], 'dp', split_axis=2, concat_axis=0, tiled...  45.7 us
    dot_general x20, matrix products, product(): return jnp.dot(left_op, right_op, preferred_element_type=jnp.float32)  31.4 us
    all_to_all x1, waiting for transfers between devices, body(): lax.all_to_all(send_grad, 'dp', split_axis=0, concat_axis=2, tiled=True)  23.2 us
    all_to_all x1, waiting for transfers between devices, body(): lax.all_to_all(send_probe, 'dp', split_axis=0, concat_axis=2, tiled=True)  23.1 us
    all_to_all x1, waiting for transfers between devices, body(): lax.all_to_all(result[None], 'dp', split_axis=2, concat_axis=0, tiled=True)  21.7 us
    all_to_all x1, starting transfers between devices, body(): lax.all_to_all(send_probe, 'dp', split_axis=0, concat_axis=2, tiled=True)  11.6 us
  transfers between devices with their start and end apart: 6, of which 5 were waited for; matrix products, arithmetic and copies ran while one was open for 5% of the time, Pallas kernels for 0%

commit v1 on v0

v1 whole, which is shorter than its diff:
```python
import functools
import math

import jax
import jax.numpy as jnp
from jax import lax
from jax.experimental import pallas as pl
from jax.experimental.pallas import tpu as pltpu
from jax.sharding import PartitionSpec as P

CLIP_RMS = 0.3
LEARN_RATE = 0.1
EPS_NORM = 1e-06

NX, NY, NC = 4, 8, 2
N = NX * NY * NC
NZ = 8
BLK = 512
HALF = 256
QUART = 128
PIECE = HALF // NY
ROWS = BLK // N
SLOTS = 8
ENTRIES = 2 * 2 * 512 * 4096

BF = jnp.bfloat16
F32 = jnp.float32
MESH = pl.DeviceIdType.MESH


def dev(y, x, c):
    return (lax.rem(y + NY, NY) * NX + lax.rem(x + NX, NX)) * NC + c


def owner_of(b):
    return (2 * b * NX + b) * NC


def mm(a, b):
    return jnp.dot(a, b, preferred_element_type=F32)


def mm_nt(a, b):
    return lax.dot_general(a, b, (((1,), (1,)), ((), ())), preferred_element_type=F32)


def mm_tn(a, b):
    return lax.dot_general(a, b, (((0,), (0,)), ((), ())), preferred_element_type=F32)


def kernel(
    table, g_hbm, f_hbm, v_hbm, p_hbm, out, nf_out,
    fac, inv, prb, send, recv,
    h, hr, xb, sbuf, yr, pb, sb, sall, zall, gbuf,
    lm, rm, km, hm, vm, ql, qr, wm, res, nf, nfr,
    load_sem, own_sem, d2d_s, d2d_r, x_s, x_r, fac_s, fac_r,
    y_s, y_r, g_s, g_r, s_s, s_r, z_s, z_r, ret_s, res_r, nf_r,
):
    i = lax.axis_index("dp")
    z = lax.axis_index("mp")
    c = lax.rem(i, NC)
    x = lax.rem(i // NC, NX)
    y = i // (NC * NX)
    is_owner = (c == 0) & (y == 2 * x)

    def remote(src, dst, ssem, rsem, d, zz=None):
        return pltpu.make_async_remote_copy(
            src_ref=src, dst_ref=dst, send_sem=ssem, recv_sem=rsem,
            device_id=(d, z if zz is None else zz), device_id_type=MESH,
        )

    def blk(o):
        return lax.rem(x + o, NX)

    loads = [
        pltpu.make_async_copy(f_hbm, fac, load_sem.at[0]),
        pltpu.make_async_copy(v_hbm, inv, load_sem.at[1]),
        pltpu.make_async_copy(p_hbm, prb, load_sem.at[2]),
    ]
    for cp in loads:
        cp.start()
    own = {}
    keep = pl.multiple_of(HALF * c, HALF)
    give = pl.multiple_of(HALF * (1 - c), HALF)
    for o in (2, 1, 3, 0):
        own[o] = pltpu.make_async_copy(g_hbm.at[blk(o), pl.ds(keep, HALF)], h.at[blk(o)], own_sem.at[o])
        own[o].start()

    bar = pltpu.get_barrier_semaphore()
    sib = dev(y, x, 1 - c)
    right, left = dev(y, x + 1, c), dev(y, x - 1, c)
    for d in [sib, right, left] + [dev(y + k, x, c) for k in range(1, NY)]:
        pl.semaphore_signal(bar, inc=1, device_id=(d, z), device_id_type=MESH)

    @pl.when(is_owner)
    def _():
        def tell(k, _):
            pl.semaphore_signal(bar, inc=1, device_id=(lax.rem(i + k, N), z), device_id_type=MESH)
            return 0

        lax.fori_loop(1, N, tell, 0)

        def tell_z(k, _):
            pl.semaphore_signal(bar, inc=1, device_id=(i, lax.rem(z + k, NZ)), device_id_type=MESH)
            return 0

        lax.fori_loop(1, NZ, tell_z, 0)
        pl.semaphore_wait(bar, 10 + 3 + NZ - 1)

    @pl.when(jnp.logical_not(is_owner))
    def _():
        pl.semaphore_wait(bar, 10 + 4)

    d2d = {}
    for o in (2, 1, 3, 0):
        d2d[o] = remote(g_hbm.at[blk(o), pl.ds(give, HALF)], hr.at[blk(o)], d2d_s.at[o], d2d_r.at[o], sib)
        d2d[o].start()

    for cp in loads:
        cp.wait()
    for b in range(NX):
        j = table[0, b]
        send[b, :, 0:1024] = fac[j]
        send[b, :, 1024:2048] = inv[j]
        send[b, :, 2048:2560] = prb[j]
    for b in range(NX):
        ow = owner_of(b)

        @pl.when(i != ow)
        def _():
            remote(send.at[b], recv.at[i], fac_s.at[b], fac_r, ow).start()

        @pl.when(i == ow)
        def _():
            pltpu.make_async_copy(send.at[b], recv.at[i], fac_r).start()

    def merge(o):
        own[o].wait()
        d2d[o].wait()
        h[blk(o)] = (h[blk(o)].astype(F32) + hr[blk(o)].astype(F32)).astype(BF)

    top, bot = pl.ds(0, QUART), pl.ds(QUART, QUART)

    def xsend(k, b, part, d):
        cp = remote(h.at[b, part], xb.at[k], x_s.at[k], x_r.at[k], d)
        cp.start()
        return cp

    merge(2)
    o_r = xsend(0, blk(2), top, right)
    o_l = xsend(1, blk(2), bot, left)
    merge(1)
    a_r = xsend(2, blk(1), bot, right)
    merge(3)
    a_l = xsend(3, blk(3), top, left)
    merge(0)
    o_r.wait_recv()
    h[blk(1), top] = (h[blk(1), top].astype(F32) + xb[0].astype(F32)).astype(BF)
    c_r = xsend(4, blk(1), top, right)
    o_l.wait_recv()
    h[blk(3), bot] = (h[blk(3), bot].astype(F32) + xb[1].astype(F32)).astype(BF)
    c_l = xsend(5, blk(3), bot, left)
    for cp in (a_r, a_l, c_r, c_l):
        cp.wait_recv()
    sbuf[top] = (h[x, top].astype(F32) + xb[3].astype(F32) + xb[4].astype(F32)).astype(BF)
    sbuf[bot] = (h[x, bot].astype(F32) + xb[2].astype(F32) + xb[5].astype(F32)).astype(BF)

    for k in (1, 7, 2, 6, 3, 5, 4):
        yy = lax.rem(y + k, NY)
        remote(sbuf.at[pl.ds(pl.multiple_of(PIECE * yy, PIECE), PIECE)], yr.at[y], y_s, y_r, dev(y + k, x, c)).start()
    yr[y] = sbuf[pl.ds(pl.multiple_of(PIECE * y, PIECE), PIECE)]
    for cp in (o_r, o_l, a_r, a_l, c_r, c_l):
        cp.wait_send()
    seven = yr.at[pl.ds(0, NY - 1)]
    pltpu.make_async_copy(seven, seven, y_r).wait()
    acc = yr[0].astype(F32)
    for k in range(1, NY):
        acc = acc + yr[k].astype(F32)
    pb[...] = acc.astype(BF)
    sq = jnp.sum(acc * acc, axis=0, keepdims=True)
    sb[...] = sq[:, 0:128] + sq[:, 128:256] + sq[:, 256:384] + sq[:, 384:512]

    mine = pl.ds(pl.multiple_of(HALF * c + PIECE * y, PIECE), PIECE)
    goal = dev(2 * x, x, 0)

    @pl.when(jnp.logical_not(is_owner))
    def _():
        remote(pb, gbuf.at[mine], g_s, g_r, goal).start()

    @pl.when(is_owner)
    def _():
        pltpu.make_async_copy(pb, gbuf.at[mine], g_r).start()

    for b in range(NX):
        ow = owner_of(b)

        @pl.when(i != ow)
        def _():
            remote(sb, sall.at[i], s_s.at[b], s_r, ow).start()

        @pl.when(i == ow)
        def _():
            pltpu.make_async_copy(sb, sall.at[i], s_r).start()

    @pl.when(is_owner)
    def _():
        pltpu.make_async_copy(recv, recv, fac_r).wait()

        def unpack(dst, lo):
            dst[...] = recv[:, :, lo : lo + BLK].astype(F32).reshape(BLK, BLK).astype(BF)

        unpack(lm, 0)
        unpack(rm, 512)
        unpack(km, 1024)
        unpack(hm, 1536)
        unpack(vm, 2048)
        wm[...] = mm_tn(km[...], vm[...]).astype(BF)
        wm[...] = mm(wm[...], hm[...]).astype(BF)
        ql[...] = mm_nt(wm[...], wm[...])
        qr[...] = mm_tn(wm[...], wm[...])

        pltpu.make_async_copy(sall, sall, s_r).wait()
        zall[z] = jnp.sum(sall[...], axis=0)

        def tell_z(k, _):
            remote(zall.at[z], zall.at[z], z_s, z_r, i, lax.rem(z + k, NZ)).start()
            return 0

        lax.fori_loop(1, NZ, tell_z, 0)
        pltpu.make_async_copy(gbuf, gbuf, g_r).wait()
        others = zall.at[pl.ds(0, NZ - 1)]
        pltpu.make_async_copy(others, others, z_r).wait()
        squares = jnp.sum(zall[...])
        clip = jnp.minimum(1.0, CLIP_RMS * math.sqrt(ENTRIES) * lax.rsqrt(jnp.full((1, 1), squares + EPS_NORM, F32)))
        gbuf[...] = (gbuf[...].astype(F32) * clip).astype(BF)
        vm[...] = mm(lm[...], gbuf[...]).astype(BF)
        wm[...] = mm_nt(vm[...], rm[...]).astype(BF)
        row = lax.broadcasted_iota(jnp.int32, (BLK, BLK), 0)
        col = lax.broadcasted_iota(jnp.int32, (BLK, BLK), 1)

        def step(factor, first, second):
            bound = jnp.max(jnp.abs(first + second)) + EPS_NORM
            change = jnp.where(row <= col, first - second, 0.0).astype(BF)
            moved = mm(change, factor)
            rate = LEARN_RATE / jnp.full((1, 1), bound, F32)
            return (factor.astype(F32) - rate * moved).astype(BF)

        km[...] = step(lm[...], mm_nt(wm[...], wm[...]), ql[...])
        hm[...] = step(rm[...], mm_tn(wm[...], wm[...]), qr[...])
        nf[:, :, 0:512] = km[...].astype(F32).reshape(N, ROWS, BLK).astype(BF)
        nf[:, :, 512:1024] = hm[...].astype(F32).reshape(N, ROWS, BLK).astype(BF)

        def back(k):
            j = (k + 1) // 2
            return lax.rem(jnp.where(lax.rem(k, 2) == 1, i + j, i + N - j), N)

        def back_nf(k, _):
            d = back(k)
            remote(nf.at[d], nfr.at[x], ret_s.at[0], nf_r.at[x], d).start()
            return 0

        lax.fori_loop(1, N, back_nf, 0)
        pltpu.make_async_copy(nf.at[i], nfr.at[x], nf_r.at[x]).start()
        vm[...] = mm_tn(km[...], km[...]).astype(BF)
        wm[...] = mm_tn(hm[...], hm[...]).astype(BF)
        vm[...] = mm(vm[...], gbuf[...]).astype(BF)
        res[...] = mm(vm[...], wm[...]).reshape(N, ROWS, BLK).astype(BF)

        def back_res(k, _):
            d = back(k)
            remote(res.at[d], out.at[x], ret_s.at[1], res_r.at[x], d).start()
            return 0

        lax.fori_loop(1, N, back_res, 0)
        pltpu.make_async_copy(res.at[i], out.at[x], res_r.at[x]).start()

    for b in range(NX):
        pltpu.make_async_copy(nfr.at[b], nfr.at[b], nf_r.at[b]).wait()
    for j in range(SLOTS):
        which = jnp.int32(0)
        hit = jnp.int32(0)
        for b in range(NX):
            same = table[0, b] == j
            which = jnp.where(same, b, which)
            hit = jnp.where(same, 1, hit)
        nf_out[j] = jnp.where(hit == 1, nfr[which].astype(F32), fac[j].astype(F32)).astype(BF)
    for b in range(NX):
        pltpu.make_async_copy(out.at[b], out.at[b], res_r.at[b]).wait()

    pltpu.make_async_copy(seven, seven, y_s).wait()
    for b in range(NX):
        ow = owner_of(b)

        @pl.when(i != ow)
        def _():
            pltpu.make_async_copy(send.at[b], send.at[b], fac_s.at[b]).wait()
            pltpu.make_async_copy(sb, sb, s_s.at[b]).wait()

    @pl.when(jnp.logical_not(is_owner))
    def _():
        pltpu.make_async_copy(pb, pb, g_s).wait()

    @pl.when(is_owner)
    def _():
        others = zall.at[pl.ds(0, NZ - 1)]
        pltpu.make_async_copy(others, others, z_s).wait()
        some = nf.at[pl.ds(0, N - 1)]
        pltpu.make_async_copy(some, some, ret_s.at[0]).wait()
        some = res.at[pl.ds(0, N - 1)]
        pltpu.make_async_copy(some, some, ret_s.at[1]).wait()


def body(partial_grads, factors, inverse_factors, probes, slot_table):
    grads = partial_grads.reshape(4, BLK, BLK)
    anywhere = pl.BlockSpec(memory_space=pl.ANY)
    vmem = pl.BlockSpec(memory_space=pltpu.VMEM)
    dma = pltpu.SemaphoreType.DMA
    V = pltpu.VMEM
    scratch = [
        V((SLOTS, ROWS, 1024), BF), V((SLOTS, ROWS, 1024), BF), V((SLOTS, ROWS, 512), BF),
        V((4, ROWS, 2560), BF), V((N, ROWS, 2560), BF),
        V((4, HALF, BLK), BF), V((4, HALF, BLK), BF), V((6, QUART, BLK), BF), V((HALF, BLK), BF),
        V((NY, PIECE, BLK), BF), V((PIECE, BLK), BF), V((1, 128), F32), V((N, 1, 128), F32),
        V((NZ, 1, 128), F32), V((BLK, BLK), BF),
        V((BLK, BLK), BF), V((BLK, BLK), BF), V((BLK, BLK), BF), V((BLK, BLK), BF), V((BLK, BLK), BF),
        V((BLK, BLK), F32), V((BLK, BLK), F32), V((BLK, BLK), BF),
        V((N, ROWS, BLK), BF), V((N, ROWS, 1024), BF), V((4, ROWS, 1024), BF),
        dma((3,)), dma((4,)), dma((4,)), dma((4,)), dma((6,)), dma((6,)), dma((4,)), dma,
        dma, dma, dma, dma, dma((4,)), dma, dma, dma, dma((2,)), dma((4,)), dma((4,)),
    ]
    out, nf = pl.pallas_call(
        kernel,
        out_shape=(
            jax.ShapeDtypeStruct((4, ROWS, BLK), BF),
            jax.ShapeDtypeStruct((SLOTS, ROWS, 1024), BF),
        ),
        in_specs=[pl.BlockSpec(memory_space=pltpu.SMEM)] + [anywhere] * 4,
        out_specs=(vmem, vmem),
        scratch_shapes=scratch,
        compiler_params=pltpu.CompilerParams(
            collective_id=1, has_side_effects=True, vmem_limit_bytes=62 * 1024 * 1024
        ),
    )(slot_table, grads, factors[0], inverse_factors[0], probes[0])
    return (out.reshape(2, 2, ROWS, BLK), nf[None])


def solution(mesh):
    return jax.shard_map(
        body,
        mesh=mesh,
        in_specs=(
            P("dp", None, None, None, "mp"),
            P("mp", None, "dp", None),
            P("mp", None, "dp", None),
            P("mp", None, "dp", None),
            P("mp", None),
        ),
        out_specs=(P(None, None, "dp", "mp"), P("mp", None, "dp", None)),
        check_vma=False,
    )
```

time: 516 us -> 77.9 us (0.15)
  waiting for transfers between devices: 268 us -> 0 us
  blocking collectives: 102 us -> 0 us
  Pallas kernels: 0 us -> 74.2 us
  local copies, waits for them, and re-layouts: 46.2 us -> 2.94 us
  starting transfers between devices: 39.9 us -> 0 us
  matrix products: 31.9 us -> 0 us
  between operations: 14.9 us -> 0.64 us
  other arithmetic: 7.96 us -> 0 us
    reduce_scatter x1 -> x0, waiting for transfers between devices: 154 us -> none  [body(): summed = lax.psum_scatter(local_sum, 'dp', scatter_dimension=2, tiled=True)]
    all_to_all x5 -> x0, waiting for transfers between devices: 114 us -> none  [the longest x1 45.7 us: body(): lax.all_to_all(moved_rows[None], 'dp', split_axis=2, concat_axis=0, tiled...]
    psum x1 -> x0, blocking collectives: 102 us -> none  [body(): squares = lax.psum(jnp.sum(gradient * gradient), ('dp', 'mp'))]
    pallas_call x0 -> x1, Pallas kernels: none -> 74.2 us  [body(): pl.pallas_call(kernel, out_shape=(jax.ShapeDtypeStruct((4, ROWS, BLK), BF...]
    all_to_all x5 -> x0, starting transfers between devices: 39.9 us -> none  [the longest x1 11.6 us: body(): lax.all_to_all(send_probe, 'dp', split_axis=0, concat_axis=2, tiled=True)]
    dot_general x22 -> x0, matrix products: 31.9 us -> none  [the longest x20 31.4 us: product(): return jnp.dot(left_op, right_op, preferred_element_type=jnp.float32)]
    while x22 -> x0, local copies, waits for them, and re-layouts: 12.1 us -> none  [the longest x2 9.58 us: body(): lax.map(run_one, (grad_in[0], state_in[0], probe_in[0]))]
    dynamic_slice x4 -> x0, local copies, waits for them, and re-layouts: 9.24 us -> none  [body(): lax.map(run_one, (grad_in[0], state_in[0], probe_in[0]))]
  transfers between devices with their start and end apart: 6 -> 0, of which waited for: 5 -> 0; matrix products, arithmetic and copies ran while one was open for 5% -> 0% of each run, Pallas kernels for 0% -> 0%
where the time goes in v1:
time: 77.9 us; the launch traced here: 77.7 us
  Pallas kernels  74.2 us (95%)
  local copies, waits for them, and re-layouts  2.94 us (4%)
    pallas_call x1, Pallas kernels, body(): pl.pallas_call(kernel, out_shape=(jax.ShapeDtypeStruct((4, ROWS, BLK), BF...  74.2 us
    unnamed x2, local copies, waits for them, and re-layouts  2.94 us

profile of v1, /device:TPU:1, one launch (start us, length us, event | category | flops | bytes accessed | tf_op | source)
XLA Modules:
  0.0 77.7 jit_solution(7511748952220479351)
XLA Ops:
  0.6 74.2 %shard_map.68 = (bf16[4,8,512]{2,1,0:T(8,128)(2,1)}, bf16[8,8,1024]{2,1,0:T(8,128)(2,1)}) custom-call(s32[1,4]{1,0:T(1,128)} %table.1, bf16[4,512,512]{2,1,0:T(8,128)(2,1)} %bitcast.6, bf16[8,8,1024]{2,1,0:T(8,128)(2,1)} %bitcast.8, bf16[8,8,1024]{2,1,0:T(8,128)(2,1)} %bitcast.9, bf16[8,8,512]{2,1,0:T(8,128)(2,1)} %bitcast.10), custom_call_target="tpu_custom_call" | custom-call | tf_op jit(solution)/shard_map/pallas_call | solution.py:331
  74.8 1.4 %copy.9 = bf16[2,2,8,512]{3,2,1,0:T(8,128)(2,1)} copy(bf16[2,2,8,512]{3,2,1,0:T(8,128)(2,1)} %bitcast.11) | data formatting | bytes 65536
  76.2 1.6 %copy.10 = bf16[1,8,8,1024]{3,2,1,0:T(8,128)(2,1)} copy(bf16[1,8,8,1024]{3,2,1,0:T(8,128)(2,1)} %bitcast.7) | data formatting | bytes 262144

commit v2 on v1

--- a/solution.py
+++ b/solution.py
@@ -32,6 +32,10 @@
     return (lax.rem(y + NY, NY) * NX + lax.rem(x + NX, NX)) * NC + c
 
 
+def width(q):
+    return BLK - 128 * q
+
+
 def owner_of(b):
     return (2 * b * NX + b) * NC
 
@@ -49,12 +53,12 @@
 
 
 def kernel(
-    table, g_hbm, f_hbm, v_hbm, p_hbm, out, nf_out,
-    fac, inv, prb, send, recv,
+    t_hbm, g_hbm, f_hbm, v_hbm, p_hbm, out, nfr,
+    table, fac, inv, prb, send, relay, recv,
     h, hr, xb, sbuf, yr, pb, sb, sall, zall, gbuf,
-    lm, rm, km, hm, vm, ql, qr, wm, res, nf, nfr,
-    load_sem, own_sem, d2d_s, d2d_r, x_s, x_r, fac_s, fac_r,
-    y_s, y_r, g_s, g_r, s_s, s_r, z_s, z_r, ret_s, res_r, nf_r,
+    lm, rm, km, hm, vm, ql, qr, wm, res, nf,
+    load_sem, own_sem, d2d_s, d2d_r, x_s, x_r, rel_s, rel_r, fac_s, fac_r,
+    y_s, y_r, g_s, g_r, s_s, s_r, z_s, z_r, nf_s, res_s, res_r, nf_r,
 ):
     i = lax.axis_index("dp")
     z = lax.axis_index("mp")
@@ -62,6 +66,11 @@
     x = lax.rem(i // NC, NX)
     y = i // (NC * NX)
     is_owner = (c == 0) & (y == 2 * x)
+    band = y // 2
+
+    def by_band(fn):
+        for q in range(4):
+            pl.when(band == q)(functools.partial(fn, q))
 
     def remote(src, dst, ssem, rsem, d, zz=None):
         return pltpu.make_async_remote_copy(
@@ -73,6 +82,7 @@
         return lax.rem(x + o, NX)
 
     loads = [
+        pltpu.make_async_copy(t_hbm, table, load_sem.at[3]),
         pltpu.make_async_copy(f_hbm, fac, load_sem.at[0]),
         pltpu.make_async_copy(v_hbm, inv, load_sem.at[1]),
         pltpu.make_async_copy(p_hbm, prb, load_sem.at[2]),
@@ -89,27 +99,18 @@
     bar = pltpu.get_barrier_semaphore()
     sib = dev(y, x, 1 - c)
     right, left = dev(y, x + 1, c), dev(y, x - 1, c)
-    for d in [sib, right, left] + [dev(y + k, x, c) for k in range(1, NY)]:
+    for d in [sib, right, left, dev(y, x + 2, c)] + [dev(y + k, x, c) for k in range(1, NY)]:
         pl.semaphore_signal(bar, inc=1, device_id=(d, z), device_id_type=MESH)
 
     @pl.when(is_owner)
     def _():
-        def tell(k, _):
-            pl.semaphore_signal(bar, inc=1, device_id=(lax.rem(i + k, N), z), device_id_type=MESH)
-            return 0
-
-        lax.fori_loop(1, N, tell, 0)
-
-        def tell_z(k, _):
+        for k in range(1, NZ):
             pl.semaphore_signal(bar, inc=1, device_id=(i, lax.rem(z + k, NZ)), device_id_type=MESH)
-            return 0
-
-        lax.fori_loop(1, NZ, tell_z, 0)
-        pl.semaphore_wait(bar, 10 + 3 + NZ - 1)
+        pl.semaphore_wait(bar, 11 + NZ - 1)
 
     @pl.when(jnp.logical_not(is_owner))
     def _():
-        pl.semaphore_wait(bar, 10 + 4)
+        pl.semaphore_wait(bar, 11)
 
     d2d = {}
     for o in (2, 1, 3, 0):
@@ -118,21 +119,40 @@
 
     for cp in loads:
         cp.wait()
-    for b in range(NX):
-        j = table[0, b]
-        send[b, :, 0:1024] = fac[j]
-        send[b, :, 1024:2048] = inv[j]
-        send[b, :, 2048:2560] = prb[j]
-    for b in range(NX):
-        ow = owner_of(b)
-
-        @pl.when(i != ow)
-        def _():
-            remote(send.at[b], recv.at[i], fac_s.at[b], fac_r, ow).start()
-
-        @pl.when(i == ow)
-        def _():
-            pltpu.make_async_copy(send.at[b], recv.at[i], fac_r).start()
+
+    def pack(q):
+        w = width(q)
+        total = 4 * w + BLK
+        for b in range(NX):
+            j = table[0, b]
+            for k, src in ((0, fac), (1, fac), (2, inv), (3, inv)):
+                lo = BLK * (k % 2)
+                send[b, :, k * w : (k + 1) * w] = src[j, :, lo + BLK - w : lo + BLK]
+            send[b, :, 4 * w : total] = prb[j]
+        for k in (1, 3, 2):
+            to = blk(k)
+            remote(
+                send.at[to, :, pl.ds(0, total)], relay.at[x, :, pl.ds(0, total)],
+                rel_s, rel_r, dev(y, x + k, c),
+            ).start()
+        relay[x, :, 0:total] = send[x, :, 0:total]
+
+    by_band(pack)
+
+    def forward(q):
+        total = 4 * width(q) + BLK
+        three = relay.at[pl.ds(0, 3), :, pl.ds(0, total)]
+        pltpu.make_async_copy(three, three, rel_r).wait()
+        src = relay.at[:, :, pl.ds(0, total)]
+        dst = recv.at[y, :, c, :, pl.ds(0, total)]
+
+        @pl.when(jnp.logical_not(is_owner))
+        def _():
+            remote(src, dst, fac_s, fac_r.at[q], dev(2 * x, x, 0)).start()
+
+        @pl.when(is_owner)
+        def _():
+            pltpu.make_async_copy(src, dst, fac_r.at[q]).start()
 
     def merge(o):
         own[o].wait()
@@ -153,6 +173,7 @@
     a_r = xsend(2, blk(1), bot, right)
     merge(3)
     a_l = xsend(3, blk(3), top, left)
+    by_band(forward)
     merge(0)
     o_r.wait_recv()
     h[blk(1), top] = (h[blk(1), top].astype(F32) + xb[0].astype(F32)).astype(BF)
@@ -204,16 +225,21 @@
 
     @pl.when(is_owner)
     def _():
-        pltpu.make_async_copy(recv, recv, fac_r).wait()
-
-        def unpack(dst, lo):
-            dst[...] = recv[:, :, lo : lo + BLK].astype(F32).reshape(BLK, BLK).astype(BF)
-
-        unpack(lm, 0)
-        unpack(rm, 512)
-        unpack(km, 1024)
-        unpack(hm, 1536)
-        unpack(vm, 2048)
+        for m in (lm, rm, km, hm):
+            for q in range(1, 4):
+                m[128 * q : 128 * (q + 1), 0 : 128 * q] = jnp.zeros((128, 128 * q), BF)
+        for q in range(4):
+            w = width(q)
+            got = recv.at[pl.ds(2 * q, 2), :, :, :, pl.ds(0, 4 * w + BLK)]
+            pltpu.make_async_copy(got, got, fac_r.at[q]).wait()
+        for q in range(4):
+            w = width(q)
+            rows = slice(128 * q, 128 * (q + 1))
+            for k, m in enumerate((lm, rm, km, hm)):
+                part = recv[2 * q : 2 * q + 2, :, :, :, k * w : (k + 1) * w]
+                m[rows, BLK - w : BLK] = part.astype(F32).reshape(128, w).astype(BF)
+            part = recv[2 * q : 2 * q + 2, :, :, :, 4 * w : 4 * w + BLK]
+            vm[rows] = part.astype(F32).reshape(128, BLK).astype(BF)
         wm[...] = mm_tn(km[...], vm[...]).astype(BF)
         wm[...] = mm(wm[...], hm[...]).astype(BF)
         ql[...] = mm_nt(wm[...], wm[...])
@@ -247,35 +273,100 @@
 
         km[...] = step(lm[...], mm_nt(wm[...], wm[...]), ql[...])
         hm[...] = step(rm[...], mm_tn(wm[...], wm[...]), qr[...])
-        nf[:, :, 0:512] = km[...].astype(F32).reshape(N, ROWS, BLK).astype(BF)
-        nf[:, :, 512:1024] = hm[...].astype(F32).reshape(N, ROWS, BLK).astype(BF)
-
-        def back(k):
-            j = (k + 1) // 2
-            return lax.rem(jnp.where(lax.rem(k, 2) == 1, i + j, i + N - j), N)
-
-        def back_nf(k, _):
-            d = back(k)
-            remote(nf.at[d], nfr.at[x], ret_s.at[0], nf_r.at[x], d).start()
+        for q in range(4):
+            w = width(q)
+            for k, m in enumerate((km, hm)):
+                part = m[128 * q : 128 * (q + 1), BLK - w : BLK]
+                nf[16 * q : 16 * (q + 1), :, k * w : (k + 1) * w] = part.astype(F32).reshape(16, ROWS, w).astype(BF)
+
+        def back(src, dst, sems, rsem, t, q, w):
+            d = 16 * q + t
+            s_ref = src.at[d, :, pl.ds(0, w)]
+            d_ref = dst.at[x, :, pl.ds(0, w)]
+
+            @pl.when(d != i)
+            def _():
+                remote(s_ref, d_ref, sems.at[q], rsem.at[x], d).start()
+
+            @pl.when(d == i)
+            def _():
+                pltpu.make_async_copy(s_ref, d_ref, rsem.at[x]).start()
+
+        def back_nf(t, _):
+            for q in range(4):
+                back(nf, nfr, nf_s, nf_r, t, q, 2 * width(q))
             return 0
 
-        lax.fori_loop(1, N, back_nf, 0)
-        pltpu.make_async_copy(nf.at[i], nfr.at[x], nf_r.at[x]).start()
+        lax.fori_loop(0, 16, back_nf, 0)
         vm[...] = mm_tn(km[...], km[...]).astype(BF)
         wm[...] = mm_tn(hm[...], hm[...]).astype(BF)
         vm[...] = mm(vm[...], gbuf[...]).astype(BF)
         res[...] = mm(vm[...], wm[...]).reshape(N, ROWS, BLK).astype(BF)
 
-        def back_res(k, _):
-            d = back(k)
-            remote(res.at[d], out.at[x], ret_s.at[1], res_r.at[x], d).start()
+        def back_res(t, _):
+            for q in range(4):
+                back(res, out, res_s, res_r, t, q, BLK)
             return 0
 
-        lax.fori_loop(1, N, back_res, 0)
-        pltpu.make_async_copy(res.at[i], out.at[x], res_r.at[x]).start()
-
+        lax.fori_loop(0, 16, back_res, 0)
+
+    def landed(q):
+        for b in range(NX):
+            part = nfr.at[b, :, pl.ds(0, 2 * width(q))]
+            pltpu.make_async_copy(part, part, nf_r.at[b]).wait()
+
+    by_band(landed)
     for b in range(NX):
-        pltpu.make_async_copy(nfr.at[b], nfr.at[b], nf_r.at[b]).wait()
+        pltpu.make_async_copy(out.at[b], out.at[b], res_r.at[b]).wait()
+
+    pltpu.make_async_copy(seven, seven, y_s).wait()
+
+    def sent(q):
+        total = 4 * width(q) + BLK
+        three = relay.at[pl.ds(0, 3), :, pl.ds(0, total)]
+        pltpu.make_async_copy(three, three, rel_s).wait()
+
+        @pl.when(jnp.logical_not(is_owner))
+        def _():
+            four = relay.at[:, :, pl.ds(0, total)]
+            pltpu.make_async_copy(four, four, fac_s).wait()
+
+    by_band(sent)
+    for b in range(NX):
+
+        @pl.when(i != owner_of(b))
+        def _():
+            pltpu.make_async_copy(sb, sb, s_s.at[b]).wait()
+
+    @pl.when(jnp.logical_not(is_owner))
+    def _():
+        pltpu.make_async_copy(pb, pb, g_s).wait()
+
+    @pl.when(is_owner)
+    def _():
+        others = zall.at[pl.ds(0, NZ - 1)]
+        pltpu.make_async_copy(others, others, z_s).wait()
+
+        def gone(src, sem, count, w):
+            some = src.at[pl.ds(0, count), :, pl.ds(0, w)]
+            pltpu.make_async_copy(some, some, sem).wait()
+
+        for q in range(4):
+
+            @pl.when(band == q)
+            def _():
+                gone(nf, nf_s.at[q], 15, 2 * width(q))
+                gone(res, res_s.at[q], 15, BLK)
+
+            @pl.when(band != q)
+            def _():
+                gone(nf, nf_s.at[q], 16, 2 * width(q))
+                gone(res, res_s.at[q], 16, BLK)
+
+
+def assemble(table, fac, rows, fresh, out, nf):
+    q = lax.axis_index("dp") // 16
+    out[...] = rows[...]
     for j in range(SLOTS):
         which = jnp.int32(0)
         hit = jnp.int32(0)
@@ -283,31 +374,18 @@
             same = table[0, b] == j
             which = jnp.where(same, b, which)
             hit = jnp.where(same, 1, hit)
-        nf_out[j] = jnp.where(hit == 1, nfr[which].astype(F32), fac[j].astype(F32)).astype(BF)
-    for b in range(NX):
-        pltpu.make_async_copy(out.at[b], out.at[b], res_r.at[b]).wait()
-
-    pltpu.make_async_copy(seven, seven, y_s).wait()
-    for b in range(NX):
-        ow = owner_of(b)
-
-        @pl.when(i != ow)
-        def _():
-            pltpu.make_async_copy(send.at[b], send.at[b], fac_s.at[b]).wait()
-            pltpu.make_async_copy(sb, sb, s_s.at[b]).wait()
-
-    @pl.when(jnp.logical_not(is_owner))
-    def _():
-        pltpu.make_async_copy(pb, pb, g_s).wait()
-
-    @pl.when(is_owner)
-    def _():
-        others = zall.at[pl.ds(0, NZ - 1)]
-        pltpu.make_async_copy(others, others, z_s).wait()
-        some = nf.at[pl.ds(0, N - 1)]
-        pltpu.make_async_copy(some, some, ret_s.at[0]).wait()
-        some = res.at[pl.ds(0, N - 1)]
-        pltpu.make_async_copy(some, some, ret_s.at[1]).wait()
+        for k in range(4):
+
+            @pl.when(q == k)
+            def _():
+                w = width(k)
+                for side in range(2):
+                    lo = BLK * side
+                    old = fac[j, :, lo + BLK - w : lo + BLK]
+                    new = fresh[which, :, side * w : (side + 1) * w]
+                    nf[j, :, lo + BLK - w : lo + BLK] = jnp.where(hit == 1, new.astype(F32), old.astype(F32)).astype(BF)
+                    if k:
+                        nf[j, :, lo : lo + BLK - w] = jnp.zeros((ROWS, BLK - w), BF)
 
 
 def body(partial_grads, factors, inverse_factors, probes, slot_table):
@@ -317,30 +395,40 @@
     dma = pltpu.SemaphoreType.DMA
     V = pltpu.VMEM
     scratch = [
+        pltpu.SMEM((1, 4), jnp.int32),
         V((SLOTS, ROWS, 1024), BF), V((SLOTS, ROWS, 1024), BF), V((SLOTS, ROWS, 512), BF),
-        V((4, ROWS, 2560), BF), V((N, ROWS, 2560), BF),
+        V((4, ROWS, 2560), BF), V((4, ROWS, 2560), BF), V((NY, NX, NC, ROWS, 2560), BF),
         V((4, HALF, BLK), BF), V((4, HALF, BLK), BF), V((6, QUART, BLK), BF), V((HALF, BLK), BF),
         V((NY, PIECE, BLK), BF), V((PIECE, BLK), BF), V((1, 128), F32), V((N, 1, 128), F32),
         V((NZ, 1, 128), F32), V((BLK, BLK), BF),
         V((BLK, BLK), BF), V((BLK, BLK), BF), V((BLK, BLK), BF), V((BLK, BLK), BF), V((BLK, BLK), BF),
         V((BLK, BLK), F32), V((BLK, BLK), F32), V((BLK, BLK), BF),
-        V((N, ROWS, BLK), BF), V((N, ROWS, 1024), BF), V((4, ROWS, 1024), BF),
-        dma((3,)), dma((4,)), dma((4,)), dma((4,)), dma((6,)), dma((6,)), dma((4,)), dma,
-        dma, dma, dma, dma, dma((4,)), dma, dma, dma, dma((2,)), dma((4,)), dma((4,)),
+        V((N, ROWS, BLK), BF), V((N, ROWS, 1024), BF),
+        dma((4,)), dma((4,)), dma((4,)), dma((4,)), dma((6,)), dma((6,)), dma, dma, dma, dma((4,)),
+        dma, dma, dma, dma, dma((4,)), dma, dma, dma, dma((4,)), dma((4,)), dma((4,)), dma((4,)),
     ]
-    out, nf = pl.pallas_call(
+    rows, fresh = pl.pallas_call(
         kernel,
         out_shape=(
             jax.ShapeDtypeStruct((4, ROWS, BLK), BF),
-            jax.ShapeDtypeStruct((SLOTS, ROWS, 1024), BF),
+            jax.ShapeDtypeStruct((4, ROWS, 1024), BF),
         ),
-        in_specs=[pl.BlockSpec(memory_space=pltpu.SMEM)] + [anywhere] * 4,
-        out_specs=(vmem, vmem),
+        in_specs=[anywhere] * 5,
+        out_specs=(anywhere, anywhere),
         scratch_shapes=scratch,
         compiler_params=pltpu.CompilerParams(
             collective_id=1, has_side_effects=True, vmem_limit_bytes=62 * 1024 * 1024
         ),
     )(slot_table, grads, factors[0], inverse_factors[0], probes[0])
+    out, nf = pl.pallas_call(
+        assemble,
+        out_shape=(
+            jax.ShapeDtypeStruct((4, ROWS, BLK), BF),
+            jax.ShapeDtypeStruct((SLOTS, ROWS, 1024), BF),
+        ),
+        in_specs=[pl.BlockSpec(memory_space=pltpu.SMEM), vmem, vmem, vmem],
+        out_specs=(vmem, vmem),
+    )(slot_table, factors[0], rows, fresh)
     return (out.reshape(2, 2, ROWS, BLK), nf[None])
 
 

time: 77.9 us -> 63.5 us (0.82)
  Pallas kernels: 74.2 us -> 62.1 us
  local copies, waits for them, and re-layouts: 2.94 us -> 0 us
    pallas_call x1, Pallas kernels: 74.2 us -> 60.3 us  [body(): pl.pallas_call(kernel, out_shape=(jax.ShapeDtypeStruct((4, ROWS, BLK), BF...]
    unnamed x2 -> x0, local copies, waits for them, and re-layouts: 2.94 us -> none
    pallas_call x0 -> x1, Pallas kernels: none -> 1.82 us  [body(): pl.pallas_call(assemble, out_shape=(jax.ShapeDtypeStruct((4, ROWS, BLK),...]
where the time goes in v2:
time: 63.5 us; the launch traced here: 62.7 us
  Pallas kernels  62.1 us (98%)
  between operations  0.64 us (1%)
    pallas_call x1, Pallas kernels, body(): pl.pallas_call(kernel, out_shape=(jax.ShapeDtypeStruct((4, ROWS, BLK), BF...  60.3 us
    pallas_call x1, Pallas kernels, body(): pl.pallas_call(assemble, out_shape=(jax.ShapeDtypeStruct((4, ROWS, BLK),...  1.82 us

profile of v2, /device:TPU:1, one launch (start us, length us, event | category | flops | bytes accessed | tf_op | source)
XLA Modules:
  0.0 62.7 jit_solution(511824861958906289)
XLA Ops:
  0.6 60.3 %shard_map.68 = (bf16[4,8,512]{2,1,0:T(8,128)(2,1)}, bf16[4,8,1024]{2,1,0:T(8,128)(2,1)}) custom-call(s32[1,4]{1,0:T(1,128)} %table.1, bf16[4,512,512]{2,1,0:T(8,128)(2,1)} %bitcast.6, bf16[8,8,1024]{2,1,0:T(8,128)(2,1)} %bitcast.7, bf16[8,8,1024]{2,1,0:T(8,128)(2,1)} %bitcast.9, bf16[8,8,512]{2,1,0:T(8,128)(2,1)} %bitcast.10), custom_call_target="tpu_custom_call" | custom-call | tf_op jit(solution)/shard_map/pallas_call | solution.py:410
  60.9 1.8 %shard_map.69 = (bf16[4,8,512]{2,1,0:T(8,128)(2,1)}, bf16[8,8,1024]{2,1,0:T(8,128)(2,1)}) custom-call(s32[1,4]{1,0:T(1,128)} %table.1, bf16[8,8,1024]{2,1,0:T(8,128)(2,1)} %bitcast.8, bf16[4,8,512]{2,1,0:T(8,128)(2,1)} %get-tuple-element.6.rows, bf16[4,8,1024]{2,1,0:T(8,128)(2,1)} %get-tuple-element.7.fresh), custom_call_target="tpu_custom_call" | custom-call | tf_op jit(solution)/shard_map/pallas_call | solution.py:423

commit v3 on v2

v3 whole, which is shorter than its diff:
```python
import functools
import math

import jax
import jax.numpy as jnp
from jax import lax
from jax.experimental import pallas as pl
from jax.experimental.pallas import tpu as pltpu
from jax.sharding import PartitionSpec as P

CLIP_RMS = 0.3
LEARN_RATE = 0.1
EPS_NORM = 1e-06

NX, NY, NC = 4, 8, 2
N = NX * NY * NC
NZ = 8
BLK = 512
HALF = 256
SETS = 2
SET = HALF // SETS
PART = SET // 2
PIECE = SET // NY
ROWS = BLK // N
SLOTS = 8
ENTRIES = 2 * 2 * 512 * 4096

BF = jnp.bfloat16
F32 = jnp.float32
MESH = pl.DeviceIdType.MESH


def dev(y, x, c):
    return (lax.rem(y + NY, NY) * NX + lax.rem(x + NX, NX)) * NC + c


def width(q):
    return BLK - 128 * q


def owner_of(b, k):
    return ((2 + 4 * k) * NX + b) * NC


def mm(a, b):
    return jnp.dot(a, b, preferred_element_type=F32)


def mm_nt(a, b):
    return lax.dot_general(a, b, (((1,), (1,)), ((), ())), preferred_element_type=F32)


def mm_tn(a, b):
    return lax.dot_general(a, b, (((0,), (0,)), ((), ())), preferred_element_type=F32)


def kernel(
    t_hbm, g_hbm, f_hbm, v_hbm, p_hbm, out, nfr,
    table, fac, inv, prb, send, relay, recv,
    h, hr, xb, sbuf, yr, y4, pb, sb, sall, zall, gbuf,
    lm, rm, km, hm, vm, ql, qr, pn, mid, wm, res, nf,
    load_sem, own_sem, d2d_s, d2d_r, x_s, x_r, rel_s, rel_r, fac_s, fac_r,
    y_s, y_r, y4_r, g_s, g_r, s_s, s_r, z_s, z_r, nf_s, res_s, res_r, nf_r,
):
    i = lax.axis_index("dp")
    z = lax.axis_index("mp")
    c = lax.rem(i, NC)
    x = lax.rem(i // NC, NX)
    y = i // (NC * NX)
    is_owner = (c == 0) & (lax.rem(y, 4) == 2)
    band = y // 2

    def to_owners(src, dst, ssem, rsem):
        for k in range(2):
            goal = dev(2 + 4 * k, x, 0)

            @pl.when(i != goal)
            def _():
                remote(src, dst, ssem.at[k], rsem, goal).start()

            @pl.when(i == goal)
            def _():
                pltpu.make_async_copy(src, dst, rsem).start()

    def owners_sent(src, ssem):
        for k in range(2):

            @pl.when(i != dev(2 + 4 * k, x, 0))
            def _():
                pltpu.make_async_copy(src, src, ssem.at[k]).wait()

    def by_band(fn):
        for q in range(4):
            pl.when(band == q)(functools.partial(fn, q))

    def remote(src, dst, ssem, rsem, d, zz=None):
        return pltpu.make_async_remote_copy(
            src_ref=src, dst_ref=dst, send_sem=ssem, recv_sem=rsem,
            device_id=(d, z if zz is None else zz), device_id_type=MESH,
        )

    def blk(o):
        return lax.rem(x + o, NX)

    loads = [
        pltpu.make_async_copy(t_hbm, table, load_sem.at[3]),
        pltpu.make_async_copy(f_hbm, fac, load_sem.at[0]),
        pltpu.make_async_copy(v_hbm, inv, load_sem.at[1]),
        pltpu.make_async_copy(p_hbm, prb, load_sem.at[2]),
    ]
    for cp in loads:
        cp.start()
    own = {}
    keep = pl.multiple_of(HALF * c, HALF)
    give = pl.multiple_of(HALF * (1 - c), HALF)
    order = ((2, 0), (2, 1), (1, 0), (3, 0), (1, 1), (3, 1), (0, 0), (0, 1))
    for o, s in order:
        own[o, s] = pltpu.make_async_copy(
            g_hbm.at[blk(o), pl.ds(keep + SET * s, SET)], h.at[blk(o), pl.ds(SET * s, SET)], own_sem.at[2 * o + s]
        )
        own[o, s].start()

    bar = pltpu.get_barrier_semaphore()
    sib = dev(y, x, 1 - c)
    right, left = dev(y, x + 1, c), dev(y, x - 1, c)
    for d in [sib, right, left, dev(y, x + 2, c)] + [dev(y + k, x, c) for k in range(1, NY)]:
        pl.semaphore_signal(bar, inc=1, device_id=(d, z), device_id_type=MESH)

    @pl.when(is_owner)
    def _():
        for k in range(1, NZ):
            pl.semaphore_signal(bar, inc=1, device_id=(i, lax.rem(z + k, NZ)), device_id_type=MESH)
        pl.semaphore_wait(bar, 11 + NZ - 1)

    @pl.when(jnp.logical_not(is_owner))
    def _():
        pl.semaphore_wait(bar, 11)

    d2d = {}
    for o, s in order:
        d2d[o, s] = remote(
            g_hbm.at[blk(o), pl.ds(give + SET * s, SET)], hr.at[blk(o), pl.ds(SET * s, SET)],
            d2d_s.at[2 * o + s], d2d_r.at[2 * o + s], sib,
        )
        d2d[o, s].start()

    for cp in loads:
        cp.wait()

    def pack(q):
        w = width(q)
        total = 4 * w + BLK
        for b in range(NX):
            j = table[0, b]
            for k, src in ((0, fac), (1, fac), (2, inv), (3, inv)):
                lo = BLK * (k % 2)
                send[b, :, k * w : (k + 1) * w] = src[j, :, lo + BLK - w : lo + BLK]
            send[b, :, 4 * w : total] = prb[j]
        for k in (1, 3, 2):
            to = blk(k)
            remote(
                send.at[to, :, pl.ds(0, total)], relay.at[x, :, pl.ds(0, total)],
                rel_s, rel_r, dev(y, x + k, c),
            ).start()
        relay[x, :, 0:total] = send[x, :, 0:total]

    by_band(pack)

    def forward(q):
        total = 4 * width(q) + BLK
        three = relay.at[pl.ds(0, 3), :, pl.ds(0, total)]
        pltpu.make_async_copy(three, three, rel_r).wait()
        src = relay.at[:, :, pl.ds(0, total)]
        dst = recv.at[y, :, c, :, pl.ds(0, total)]

        to_owners(src, dst, fac_s, fac_r.at[q])

    def merge(o, s):
        own[o, s].wait()
        d2d[o, s].wait()
        part = pl.ds(SET * s, SET)
        h[blk(o), part] = (h[blk(o), part].astype(F32) + hr[blk(o), part].astype(F32)).astype(BF)

    def top(s):
        return pl.ds(SET * s, PART)

    def bot(s):
        return pl.ds(SET * s + PART, PART)

    xs = {}

    def xsend(k, s, b, part, d):
        n = 6 * s + k
        xs[k, s] = remote(h.at[b, part], xb.at[n], x_s.at[n], x_r.at[n], d)
        xs[k, s].start()

    def plus(k, s, b, part):
        xs[k, s].wait_recv()
        h[b, part] = (h[b, part].astype(F32) + xb[6 * s + k].astype(F32)).astype(BF)

    for s in range(SETS):
        merge(2, s)
        xsend(0, s, blk(2), top(s), right)
        xsend(1, s, blk(2), bot(s), left)
    merge(1, 0)
    xsend(2, 0, blk(1), bot(0), right)
    merge(3, 0)
    xsend(3, 0, blk(3), top(0), left)
    merge(1, 1)
    merge(3, 1)
    by_band(forward)
    for s in range(SETS):
        plus(0, s, blk(1), top(s))
        xsend(4, s, blk(1), top(s), right)
        plus(1, s, blk(3), bot(s))
        xsend(5, s, blk(3), bot(s), left)
        if s == 0:
            xsend(2, 1, blk(1), bot(1), right)
            xsend(3, 1, blk(3), top(1), left)
    merge(0, 0)
    merge(0, 1)

    def piece(s, k):
        return pl.ds(SET * s + pl.multiple_of(PIECE * lax.rem(y + k, NY), PIECE), PIECE)

    def ysend(s, slot, k):
        remote(sbuf.at[piece(s, k)], yr.at[s, slot], y_s.at[s], y_r.at[s], dev(y + k, x, c)).start()

    far = {}
    for s in range(SETS):
        for k in (2, 3, 4, 5):
            xs[k, s].wait_recv()
        n = 6 * s
        sbuf[top(s)] = (h[x, top(s)].astype(F32) + xb[n + 3].astype(F32) + xb[n + 4].astype(F32)).astype(BF)
        sbuf[bot(s)] = (h[x, bot(s)].astype(F32) + xb[n + 2].astype(F32) + xb[n + 5].astype(F32)).astype(BF)
        far[s] = remote(sbuf.at[piece(s, 4)], y4.at[s], y_s.at[s], y4_r.at[s], dev(y + 7, x, c))
        far[s].start()
        for slot, k in enumerate((3, 6, 2, 7, 1)):
            ysend(s, slot, k)

    for s in range(SETS):
        far[s].wait_recv()
        sbuf[piece(s, 5)] = (sbuf[piece(s, 5)].astype(F32) + y4[s].astype(F32)).astype(BF)
        ysend(s, 5, 5)
    for cp in xs.values():
        cp.wait_send()
    sq = jnp.zeros((1, BLK), F32)

    def ysum(s):
        pltpu.make_async_copy(yr.at[s], yr.at[s], y_r.at[s]).wait()
        acc = sbuf[piece(s, 0)].astype(F32)
        for k in range(NY - 2):
            acc = acc + yr[s, k].astype(F32)
        pb[s] = acc.astype(BF)
        return jnp.sum(acc * acc, axis=0, keepdims=True)

    def pieces(s):
        mine = pl.ds(pl.multiple_of(HALF * c + SET * s + PIECE * y, PIECE), PIECE)
        to_owners(pb.at[s], gbuf.at[mine], g_s.at[s], g_r)

    sq = ysum(0)
    pieces(0)
    sq = sq + ysum(1)
    sb[...] = sq[:, 0:128] + sq[:, 128:256] + sq[:, 256:384] + sq[:, 384:512]

    for b in range(NX):
        for k in range(2):
            ow = owner_of(b, k)

            @pl.when(i != ow)
            def _():
                remote(sb, sall.at[y, x, c], s_s.at[2 * b + k], s_r, ow).start()

            @pl.when(i == ow)
            def _():
                pltpu.make_async_copy(sb, sall.at[y, x, c], s_r).start()

    pieces(1)

    @pl.when(is_owner)
    def _():
        for m in (lm, rm, km, hm):
            for q in range(1, 4):
                m[128 * q : 128 * (q + 1), 0 : 128 * q] = jnp.zeros((128, 128 * q), BF)
        for q in range(4):
            w = width(q)
            got = recv.at[pl.ds(2 * q, 2), :, :, :, pl.ds(0, 4 * w + BLK)]
            pltpu.make_async_copy(got, got, fac_r.at[q]).wait()
        for q in range(4):
            w = width(q)
            rows = slice(128 * q, 128 * (q + 1))
            for k, m in enumerate((lm, rm, km, hm)):
                part = recv[2 * q : 2 * q + 2, :, :, :, k * w : (k + 1) * w]
                m[rows, BLK - w : BLK] = part.astype(F32).reshape(128, w).astype(BF)
            part = recv[2 * q : 2 * q + 2, :, :, :, 4 * w : 4 * w + BLK]
            vm[rows] = part.astype(F32).reshape(128, BLK).astype(BF)
        row = lax.broadcasted_iota(jnp.int32, (BLK, BLK), 0)
        col = lax.broadcasted_iota(jnp.int32, (BLK, BLK), 1)

        def full(v):
            return jnp.full((1, 1), v, F32)

        def upper(m):
            return jnp.where(row <= col, m, 0.0).astype(BF)

        def scaled(m):
            top_value = jnp.maximum(jnp.max(jnp.abs(m)), 1e-30)
            return (m * (1.0 / full(top_value))).astype(BF), top_value

        wm[...] = mm_tn(km[...], vm[...]).astype(BF)
        wm[...], q_top = scaled(mm(wm[...], hm[...]))
        for side, (m, gram) in enumerate(((lm, mm_nt), (rm, mm_tn))):
            value = gram(wm[...], wm[...])
            (ql, qr)[side][...] = value
            mid[side] = mm(upper(value), m[...])

        pltpu.make_async_copy(sall, sall, s_r).wait()
        zall[z] = jnp.sum(sall[...], axis=(0, 1, 2))
        local = jnp.sum(sall[:, x])

        def tell_z(k, _):
            remote(zall.at[z], zall.at[z], z_s, z_r, i, lax.rem(z + k, NZ)).start()
            return 0

        lax.fori_loop(1, NZ, tell_z, 0)
        limit = CLIP_RMS * math.sqrt(ENTRIES)

        def clip_of(squares):
            return jnp.minimum(1.0, limit * lax.rsqrt(full(squares + EPS_NORM)))

        pltpu.make_async_copy(gbuf, gbuf, g_r).wait()
        first_clip = clip_of(local)
        gbuf[...] = (gbuf[...].astype(F32) * first_clip).astype(BF)
        vm[...] = mm(lm[...], gbuf[...]).astype(BF)
        wm[...], p_top = scaled(mm_nt(vm[...], rm[...]))
        for side, (m, gram) in enumerate(((lm, mm_nt), (rm, mm_tn))):
            value = gram(wm[...], wm[...])
            pn[side] = value
            mid[2 + side] = mm(upper(value), m[...])
        others = zall.at[pl.ds(0, NZ - 1)]
        pltpu.make_async_copy(others, others, z_r).wait()
        ratio = clip_of(jnp.sum(zall[...])) / first_clip
        gbuf[...] = (gbuf[...].astype(F32) * ratio).astype(BF)
        p_scale = (ratio * p_top) * (ratio * p_top)
        q_scale = full(q_top) * full(q_top)
        for side, (m, q_ref, new) in enumerate(((lm, ql, km), (rm, qr, hm))):
            bound = jnp.max(jnp.abs(p_scale * pn[side] + q_scale * q_ref[...])) + EPS_NORM
            rate = LEARN_RATE / full(bound)
            moved = (rate * p_scale) * mid[2 + side] - (rate * q_scale) * mid[side]
            new[...] = (m[...].astype(F32) - moved).astype(BF)
        for q in range(4):
            w = width(q)
            for k, m in enumerate((km, hm)):
                part = m[128 * q : 128 * (q + 1), BLK - w : BLK]
                nf[16 * q : 16 * (q + 1), :, k * w : (k + 1) * w] = part.astype(F32).reshape(16, ROWS, w).astype(BF)

        def back(src, dst, sems, rsem, widths):
            def column(t, _):
                for yy in range(NY):
                    gap = lax.rem(yy + NY - y, NY)
                    odd = lax.rem(t, 2)
                    w = widths[yy // 2]
                    d = NX * NC * yy + t
                    s_ref = src.at[d, :, pl.ds(0, w)]
                    d_ref = dst.at[x, :, pl.ds(0, w)]
                    near = (gap <= 1) | (gap == 7) | ((gap == 2) & (odd == 0)) | ((gap == 6) & (odd == 1))

                    @pl.when(near & (d != i))
                    def _():
                        remote(s_ref, d_ref, sems.at[yy], rsem.at[x], d).start()

                    @pl.when(d == i)
                    def _():
                        pltpu.make_async_copy(s_ref, d_ref, rsem.at[x]).start()

                return 0

            lax.fori_loop(0, NX * NC, column, 0)

        nf_widths = [2 * width(q) for q in range(4)]
        res_widths = [BLK] * 4
        back(nf, nfr, nf_s, nf_r, nf_widths)
        vm[...] = mm_tn(km[...], km[...]).astype(BF)
        wm[...] = mm_tn(hm[...], hm[...]).astype(BF)
        vm[...] = mm(vm[...], gbuf[...]).astype(BF)
        res[...] = mm(vm[...], wm[...]).reshape(N, ROWS, BLK).astype(BF)

        back(res, out, res_s, res_r, res_widths)

    def landed(q):
        for b in range(NX):
            part = nfr.at[b, :, pl.ds(0, 2 * width(q))]
            pltpu.make_async_copy(part, part, nf_r.at[b]).wait()

    by_band(landed)
    for b in range(NX):
        pltpu.make_async_copy(out.at[b], out.at[b], res_r.at[b]).wait()

    seven = sbuf.at[pl.ds(0, 7 * PIECE)]
    for s in range(SETS):
        pltpu.make_async_copy(seven, seven, y_s.at[s]).wait()

    def sent(q):
        total = 4 * width(q) + BLK
        three = relay.at[pl.ds(0, 3), :, pl.ds(0, total)]
        pltpu.make_async_copy(three, three, rel_s).wait()

        owners_sent(relay.at[:, :, pl.ds(0, total)], fac_s)

    by_band(sent)
    for s in range(SETS):
        owners_sent(pb.at[s], g_s.at[s])
    for b in range(NX):
        for k in range(2):

            @pl.when(i != owner_of(b, k))
            def _():
                pltpu.make_async_copy(sb, sb, s_s.at[2 * b + k]).wait()

    @pl.when(is_owner)
    def _():
        others = zall.at[pl.ds(0, NZ - 1)]
        pltpu.make_async_copy(others, others, z_s).wait()

        nf_widths = [2 * width(q) for q in range(4)]

        def gone(src, sem, count, w):
            some = src.at[pl.ds(0, count), :, pl.ds(0, w)]
            pltpu.make_async_copy(some, some, sem).wait()

        for yy in range(NY):
            gap = lax.rem(yy + NY - y, NY)
            for count, here in ((7, gap == 0), (8, (gap == 1) | (gap == 7)), (4, (gap == 2) | (gap == 6))):

                @pl.when(here)
                def _():
                    gone(nf, nf_s.at[yy], count, nf_widths[yy // 2])
                    gone(res, res_s.at[yy], count, BLK)


def assemble(table, fac, rows, fresh, out, nf):
    q = lax.axis_index("dp") // 16
    out[...] = rows[...]
    for j in range(SLOTS):
        which = jnp.int32(0)
        hit = jnp.int32(0)
        for b in range(NX):
            same = table[0, b] == j
            which = jnp.where(same, b, which)
            hit = jnp.where(same, 1, hit)
        for k in range(4):

            @pl.when(q == k)
            def _():
                w = width(k)
                for side in range(2):
                    lo = BLK * side
                    old = fac[j, :, lo + BLK - w : lo + BLK]
                    new = fresh[which, :, side * w : (side + 1) * w]
                    nf[j, :, lo + BLK - w : lo + BLK] = jnp.where(hit == 1, new.astype(F32), old.astype(F32)).astype(BF)
                    if k:
                        nf[j, :, lo : lo + BLK - w] = jnp.zeros((ROWS, BLK - w), BF)


def body(partial_grads, factors, inverse_factors, probes, slot_table):
    grads = partial_grads.reshape(4, BLK, BLK)
    anywhere = pl.BlockSpec(memory_space=pl.ANY)
    vmem = pl.BlockSpec(memory_space=pltpu.VMEM)
    dma = pltpu.SemaphoreType.DMA
    V = pltpu.VMEM
    scratch = [
        pltpu.SMEM((1, 4), jnp.int32),
        V((SLOTS, ROWS, 1024), BF), V((SLOTS, ROWS, 1024), BF), V((SLOTS, ROWS, 512), BF),
        V((4, ROWS, 2560), BF), V((4, ROWS, 2560), BF), V((NY, NX, NC, ROWS, 2560), BF),
        V((4, HALF, BLK), BF), V((4, HALF, BLK), BF), V((6 * SETS, PART, BLK), BF), V((HALF, BLK), BF),
        V((SETS, NY - 2, PIECE, BLK), BF), V((SETS, PIECE, BLK), BF), V((SETS, PIECE, BLK), BF), V((1, 128), F32), V((NY, NX, NC, 1, 128), F32),
        V((NZ, 1, 128), F32), V((BLK, BLK), BF),
        V((BLK, BLK), BF), V((BLK, BLK), BF), V((BLK, BLK), BF), V((BLK, BLK), BF), V((BLK, BLK), BF),
        V((BLK, BLK), F32), V((BLK, BLK), F32), V((2, BLK, BLK), F32), V((4, BLK, BLK), F32), V((BLK, BLK), BF),
        V((N, ROWS, BLK), BF), V((N, ROWS, 1024), BF),
        dma((4,)), dma((8,)), dma((8,)), dma((8,)), dma((12,)), dma((12,)), dma, dma, dma((2,)), dma((4,)),
        dma((2,)), dma((2,)), dma((2,)), dma((2, 2)), dma, dma((8,)), dma, dma, dma, dma((8,)), dma((8,)), dma((4,)), dma((4,)),
    ]
    rows, fresh = pl.pallas_call(
        kernel,
        out_shape=(
            jax.ShapeDtypeStruct((4, ROWS, BLK), BF),
            jax.ShapeDtypeStruct((4, ROWS, 1024), BF),
        ),
        in_specs=[anywhere] * 5,
        out_specs=(anywhere, anywhere),
        scratch_shapes=scratch,
        compiler_params=pltpu.CompilerParams(
            collective_id=1, has_side_effects=True, vmem_limit_bytes=62 * 1024 * 1024
        ),
    )(slot_table, grads, factors[0], inverse_factors[0], probes[0])
    out, nf = pl.pallas_call(
        assemble,
        out_shape=(
            jax.ShapeDtypeStruct((4, ROWS, BLK), BF),
            jax.ShapeDtypeStruct((SLOTS, ROWS, 1024), BF),
        ),
        in_specs=[pl.BlockSpec(memory_space=pltpu.SMEM), vmem, vmem, vmem],
        out_specs=(vmem, vmem),
    )(slot_table, factors[0], rows, fresh)
    return (out.reshape(2, 2, ROWS, BLK), nf[None])


def solution(mesh):
    return jax.shard_map(
        body,
        mesh=mesh,
        in_specs=(
            P("dp", None, None, None, "mp"),
            P("mp", None, "dp", None),
            P("mp", None, "dp", None),
            P("mp", None, "dp", None),
            P("mp", None),
        ),
        out_specs=(P(None, None, "dp", "mp"), P("mp", None, "dp", None)),
        check_vma=False,
    )
```

time: 63.5 us -> 57 us (0.90)
  Pallas kernels: 62.1 us -> 56.2 us
    pallas_call x1, Pallas kernels: 60.3 us -> 54.4 us  [body(): pl.pallas_call(kernel, out_shape=(jax.ShapeDtypeStruct((4, ROWS, BLK), BF...]
where the time goes in v3:
time: 57 us; the launch traced here: 56.8 us
  Pallas kernels  56.2 us (99%)
  between operations  0.64 us (1%)
    pallas_call x1, Pallas kernels, body(): pl.pallas_call(kernel, out_shape=(jax.ShapeDtypeStruct((4, ROWS, BLK), BF...  54.4 us
    pallas_call x1, Pallas kernels, body(): pl.pallas_call(assemble, out_shape=(jax.ShapeDtypeStruct((4, ROWS, BLK),...  1.82 us

profile of v3, /device:TPU:1, one launch (start us, length us, event | category | flops | bytes accessed | tf_op | source)
XLA Modules:
  0.0 56.8 jit_solution(764856714766475818)
XLA Ops:
  0.6 54.4 %shard_map.68 = (bf16[4,8,512]{2,1,0:T(8,128)(2,1)}, bf16[4,8,1024]{2,1,0:T(8,128)(2,1)}) custom-call(s32[1,4]{1,0:T(1,128)} %table.1, bf16[4,512,512]{2,1,0:T(8,128)(2,1)} %bitcast.6, bf16[8,8,1024]{2,1,0:T(8,128)(2,1)} %bitcast.7, bf16[8,8,1024]{2,1,0:T(8,128)(2,1)} %bitcast.9, bf16[8,8,512]{2,1,0:T(8,128)(2,1)} %bitcast.10), custom_call_target="tpu_custom_call" | custom-call | tf_op jit(solution)/shard_map/pallas_call | solution.py:484
  55.0 1.8 %shard_map.69 = (bf16[4,8,512]{2,1,0:T(8,128)(2,1)}, bf16[8,8,1024]{2,1,0:T(8,128)(2,1)}) custom-call(s32[1,4]{1,0:T(1,128)} %table.1, bf16[8,8,1024]{2,1,0:T(8,128)(2,1)} %bitcast.8, bf16[4,8,512]{2,1,0:T(8,128)(2,1)} %get-tuple-element.6.rows, bf16[4,8,1024]{2,1,0:T(8,128)(2,1)} %get-tuple-element.7.fresh), custom_call_target="tpu_custom_call" | custom-call | tf_op jit(solution)/shard_map/pallas_call | solution.py:497

commit v4 on v3

--- a/solution.py
+++ b/solution.py
@@ -55,10 +55,10 @@
 
 
 def kernel(
-    t_hbm, g_hbm, f_hbm, v_hbm, p_hbm, out, nfr,
+    t_hbm, g_hbm, f_hbm, v_hbm, p_hbm, out, nf_hbm,
     table, fac, inv, prb, send, relay, recv,
     h, hr, xb, sbuf, yr, y4, pb, sb, sall, zall, gbuf,
-    lm, rm, km, hm, vm, ql, qr, pn, mid, wm, res, nf,
+    lm, rm, km, hm, vm, ql, qr, pn, mid, wm, res, nf, nfr, full_nf, out_sem,
     load_sem, own_sem, d2d_s, d2d_r, x_s, x_r, rel_s, rel_r, fac_s, fac_r,
     y_s, y_r, y4_r, g_s, g_r, s_s, s_r, z_s, z_r, nf_s, res_s, res_r, nf_r,
 ):
@@ -226,30 +226,34 @@
     def ysend(s, slot, k):
         remote(sbuf.at[piece(s, k)], yr.at[s, slot], y_s.at[s], y_r.at[s], dev(y + k, x, c)).start()
 
-    far = {}
     for s in range(SETS):
         for k in (2, 3, 4, 5):
             xs[k, s].wait_recv()
         n = 6 * s
         sbuf[top(s)] = (h[x, top(s)].astype(F32) + xb[n + 3].astype(F32) + xb[n + 4].astype(F32)).astype(BF)
         sbuf[bot(s)] = (h[x, bot(s)].astype(F32) + xb[n + 2].astype(F32) + xb[n + 5].astype(F32)).astype(BF)
-        far[s] = remote(sbuf.at[piece(s, 4)], y4.at[s], y_s.at[s], y4_r.at[s], dev(y + 7, x, c))
-        far[s].start()
+        if s == 0:
+            far = remote(sbuf.at[piece(s, 4)], y4, y_s.at[s], y4_r, dev(y + 7, x, c))
+            far.start()
+        else:
+            ysend(s, 6, 4)
+            ysend(s, 5, 5)
         for slot, k in enumerate((3, 6, 2, 7, 1)):
             ysend(s, slot, k)
 
-    for s in range(SETS):
-        far[s].wait_recv()
-        sbuf[piece(s, 5)] = (sbuf[piece(s, 5)].astype(F32) + y4[s].astype(F32)).astype(BF)
-        ysend(s, 5, 5)
+    far.wait_recv()
+    sbuf[piece(0, 5)] = (sbuf[piece(0, 5)].astype(F32) + y4[...].astype(F32)).astype(BF)
+    ysend(0, 5, 5)
     for cp in xs.values():
         cp.wait_send()
     sq = jnp.zeros((1, BLK), F32)
 
     def ysum(s):
-        pltpu.make_async_copy(yr.at[s], yr.at[s], y_r.at[s]).wait()
+        count = NY - 2 + s
+        got = yr.at[s, pl.ds(0, count)]
+        pltpu.make_async_copy(got, got, y_r.at[s]).wait()
         acc = sbuf[piece(s, 0)].astype(F32)
-        for k in range(NY - 2):
+        for k in range(count):
             acc = acc + yr[s, k].astype(F32)
         pb[s] = acc.astype(BF)
         return jnp.sum(acc * acc, axis=0, keepdims=True)
@@ -344,10 +348,14 @@
         p_scale = (ratio * p_top) * (ratio * p_top)
         q_scale = full(q_top) * full(q_top)
         for side, (m, q_ref, new) in enumerate(((lm, ql, km), (rm, qr, hm))):
-            bound = jnp.max(jnp.abs(p_scale * pn[side] + q_scale * q_ref[...])) + EPS_NORM
+            parts = [(slice(128 * q, 128 * (q + 1)), slice(128 * q, BLK)) for q in range(4)]
+            tops = [jnp.max(jnp.abs(p_scale * pn[side, r, k] + q_scale * q_ref[r, k])) for r, k in parts]
+            bound = functools.reduce(jnp.maximum, tops) + EPS_NORM
             rate = LEARN_RATE / full(bound)
-            moved = (rate * p_scale) * mid[2 + side] - (rate * q_scale) * mid[side]
-            new[...] = (m[...].astype(F32) - moved).astype(BF)
+            p_rate, q_rate = rate * p_scale, rate * q_scale
+            for r, k in parts:
+                moved = p_rate * mid[2 + side, r, k] - q_rate * mid[side, r, k]
+                new[r, k] = (m[r, k].astype(F32) - moved).astype(BF)
         for q in range(4):
             w = width(q)
             for k, m in enumerate((km, hm)):
@@ -355,27 +363,26 @@
                 nf[16 * q : 16 * (q + 1), :, k * w : (k + 1) * w] = part.astype(F32).reshape(16, ROWS, w).astype(BF)
 
         def back(src, dst, sems, rsem, widths):
-            def column(t, _):
-                for yy in range(NY):
-                    gap = lax.rem(yy + NY - y, NY)
-                    odd = lax.rem(t, 2)
-                    w = widths[yy // 2]
-                    d = NX * NC * yy + t
-                    s_ref = src.at[d, :, pl.ds(0, w)]
-                    d_ref = dst.at[x, :, pl.ds(0, w)]
-                    near = (gap <= 1) | (gap == 7) | ((gap == 2) & (odd == 0)) | ((gap == 6) & (odd == 1))
-
-                    @pl.when(near & (d != i))
-                    def _():
-                        remote(s_ref, d_ref, sems.at[yy], rsem.at[x], d).start()
-
-                    @pl.when(d == i)
-                    def _():
-                        pltpu.make_async_copy(s_ref, d_ref, rsem.at[x]).start()
-
-                return 0
-
-            lax.fori_loop(0, NX * NC, column, 0)
+            def refs(d, row):
+                w = widths[row // 2]
+                return src.at[d, :, pl.ds(0, w)], dst.at[x, :, pl.ds(0, w)]
+
+            def rows_from(base):
+                for t in range(NX * NC):
+                    for step in (1, -1, 2, -2, 0):
+                        row = (base + step) % NY
+                        if (step == 2 and t % 2 == 1) or (step == -2 and t % 2 == 0):
+                            continue
+                        d = NX * NC * row + t
+                        if step == 0 and t % 2 == 0:
+                            if t == 0:
+                                pltpu.make_async_copy(*refs(i, row), rsem.at[x]).start()
+                                continue
+                            d = dev(row, x + t // 2, 0)
+                        remote(*refs(d, row), sems.at[row], rsem.at[x], d).start()
+
+            for base in (2, 6):
+                pl.when(y == base)(functools.partial(rows_from, base))
 
         nf_widths = [2 * width(q) for q in range(4)]
         res_widths = [BLK] * 4
@@ -391,10 +398,30 @@
         for b in range(NX):
             part = nfr.at[b, :, pl.ds(0, 2 * width(q))]
             pltpu.make_async_copy(part, part, nf_r.at[b]).wait()
+        w = width(q)
+        for j in range(SLOTS):
+            which = jnp.int32(0)
+            hit = jnp.int32(0)
+            for b in range(NX):
+                same = table[0, b] == j
+                which = jnp.where(same, b, which)
+                hit = jnp.where(same, 1, hit)
+            for side in range(2):
+                lo = BLK * side
+                old = fac[j, :, lo + BLK - w : lo + BLK]
+                new = nfr[which, :, side * w : (side + 1) * w]
+                full_nf[j, :, lo + BLK - w : lo + BLK] = jnp.where(
+                    hit == 1, new.astype(F32), old.astype(F32)
+                ).astype(BF)
+                if q:
+                    full_nf[j, :, lo : lo + BLK - w] = jnp.zeros((ROWS, BLK - w), BF)
 
     by_band(landed)
+    finish = pltpu.make_async_copy(full_nf, nf_hbm, out_sem)
+    finish.start()
     for b in range(NX):
         pltpu.make_async_copy(out.at[b], out.at[b], res_r.at[b]).wait()
+    finish.wait()
 
     seven = sbuf.at[pl.ds(0, 7 * PIECE)]
     for s in range(SETS):
@@ -438,34 +465,21 @@
                     gone(res, res_s.at[yy], count, BLK)
 
 
-def assemble(table, fac, rows, fresh, out, nf):
-    q = lax.axis_index("dp") // 16
-    out[...] = rows[...]
-    for j in range(SLOTS):
-        which = jnp.int32(0)
-        hit = jnp.int32(0)
-        for b in range(NX):
-            same = table[0, b] == j
-            which = jnp.where(same, b, which)
-            hit = jnp.where(same, 1, hit)
-        for k in range(4):
-
-            @pl.when(q == k)
-            def _():
-                w = width(k)
-                for side in range(2):
-                    lo = BLK * side
-                    old = fac[j, :, lo + BLK - w : lo + BLK]
-                    new = fresh[which, :, side * w : (side + 1) * w]
-                    nf[j, :, lo + BLK - w : lo + BLK] = jnp.where(hit == 1, new.astype(F32), old.astype(F32)).astype(BF)
-                    if k:
-                        nf[j, :, lo : lo + BLK - w] = jnp.zeros((ROWS, BLK - w), BF)
+def hand_on(rows_in, nf_in, rows_out, nf_out, rows, nf, sems):
+    ins = [pltpu.make_async_copy(nf_in, nf, sems.at[0]), pltpu.make_async_copy(rows_in, rows, sems.at[1])]
+    outs = [pltpu.make_async_copy(nf, nf_out, sems.at[2]), pltpu.make_async_copy(rows, rows_out, sems.at[3])]
+    for cp in ins:
+        cp.start()
+    for first, second in zip(ins, outs):
+        first.wait()
+        second.start()
+    for cp in outs:
+        cp.wait()
 
 
 def body(partial_grads, factors, inverse_factors, probes, slot_table):
     grads = partial_grads.reshape(4, BLK, BLK)
     anywhere = pl.BlockSpec(memory_space=pl.ANY)
-    vmem = pl.BlockSpec(memory_space=pltpu.VMEM)
     dma = pltpu.SemaphoreType.DMA
     V = pltpu.VMEM
     scratch = [
@@ -473,20 +487,21 @@
         V((SLOTS, ROWS, 1024), BF), V((SLOTS, ROWS, 1024), BF), V((SLOTS, ROWS, 512), BF),
         V((4, ROWS, 2560), BF), V((4, ROWS, 2560), BF), V((NY, NX, NC, ROWS, 2560), BF),
         V((4, HALF, BLK), BF), V((4, HALF, BLK), BF), V((6 * SETS, PART, BLK), BF), V((HALF, BLK), BF),
-        V((SETS, NY - 2, PIECE, BLK), BF), V((SETS, PIECE, BLK), BF), V((SETS, PIECE, BLK), BF), V((1, 128), F32), V((NY, NX, NC, 1, 128), F32),
+        V((SETS, NY - 1, PIECE, BLK), BF), V((PIECE, BLK), BF), V((SETS, PIECE, BLK), BF), V((1, 128), F32), V((NY, NX, NC, 1, 128), F32),
         V((NZ, 1, 128), F32), V((BLK, BLK), BF),
         V((BLK, BLK), BF), V((BLK, BLK), BF), V((BLK, BLK), BF), V((BLK, BLK), BF), V((BLK, BLK), BF),
         V((BLK, BLK), F32), V((BLK, BLK), F32), V((2, BLK, BLK), F32), V((4, BLK, BLK), F32), V((BLK, BLK), BF),
-        V((N, ROWS, BLK), BF), V((N, ROWS, 1024), BF),
+        V((N, ROWS, BLK), BF), V((N, ROWS, 1024), BF), V((4, ROWS, 1024), BF), V((SLOTS, ROWS, 1024), BF), dma,
         dma((4,)), dma((8,)), dma((8,)), dma((8,)), dma((12,)), dma((12,)), dma, dma, dma((2,)), dma((4,)),
-        dma((2,)), dma((2,)), dma((2,)), dma((2, 2)), dma, dma((8,)), dma, dma, dma, dma((8,)), dma((8,)), dma((4,)), dma((4,)),
+        dma((2,)), dma((2,)), dma, dma((2, 2)), dma, dma((8,)), dma, dma, dma, dma((8,)), dma((8,)), dma((4,)), dma((4,)),
     ]
+    shapes = (
+        jax.ShapeDtypeStruct((4, ROWS, BLK), BF),
+        jax.ShapeDtypeStruct((SLOTS, ROWS, 1024), BF),
+    )
     rows, fresh = pl.pallas_call(
         kernel,
-        out_shape=(
-            jax.ShapeDtypeStruct((4, ROWS, BLK), BF),
-            jax.ShapeDtypeStruct((4, ROWS, 1024), BF),
-        ),
+        out_shape=shapes,
         in_specs=[anywhere] * 5,
         out_specs=(anywhere, anywhere),
         scratch_shapes=scratch,
@@ -495,14 +510,12 @@
         ),
     )(slot_table, grads, factors[0], inverse_factors[0], probes[0])
     out, nf = pl.pallas_call(
-        assemble,
-        out_shape=(
-            jax.ShapeDtypeStruct((4, ROWS, BLK), BF),
-            jax.ShapeDtypeStruct((SLOTS, ROWS, 1024), BF),
-        ),
-        in_specs=[pl.BlockSpec(memory_space=pltpu.SMEM), vmem, vmem, vmem],
-        out_specs=(vmem, vmem),
-    )(slot_table, factors[0], rows, fresh)
+        hand_on,
+        out_shape=shapes,
+        in_specs=[anywhere] * 2,
+        out_specs=(anywhere, anywhere),
+        scratch_shapes=[V((4, ROWS, BLK), BF), V((SLOTS, ROWS, 1024), BF), dma((4,))],
+    )(rows, fresh)
     return (out.reshape(2, 2, ROWS, BLK), nf[None])
 
 

time: 57 us -> 56.2 us (0.986)
  Pallas kernels: 56.2 us -> 55.4 us
    pallas_call x2, Pallas kernels: 56.2 us -> 55.4 us  [the longest x1 53.8 us: body(): pl.pallas_call(kernel, out_shape=shapes, in_specs=[anywhere] * 5, out_spe...]
where the time goes in v4:
time: 56.2 us; the launch traced here: 56 us
  Pallas kernels  55.4 us (99%)
  between operations  0.64 us (1%)
    pallas_call x1, Pallas kernels, body(): pl.pallas_call(kernel, out_shape=shapes, in_specs=[anywhere] * 5, out_spe...  53.8 us
    pallas_call x1, Pallas kernels, body(): pl.pallas_call(hand_on, out_shape=shapes, in_specs=[anywhere] * 2, out_sp...  1.6 us

profile of v4, /device:TPU:1, one launch (start us, length us, event | category | flops | bytes accessed | tf_op | source)
XLA Modules:
  0.0 56.0 jit_solution(4515632846343358201)
XLA Ops:
  0.6 53.8 %shard_map.68 = (bf16[4,8,512]{2,1,0:T(8,128)(2,1)}, bf16[8,8,1024]{2,1,0:T(8,128)(2,1)}) custom-call(s32[1,4]{1,0:T(1,128)} %t_hbm.1, bf16[4,512,512]{2,1,0:T(8,128)(2,1)} %bitcast.6, bf16[8,8,1024]{2,1,0:T(8,128)(2,1)} %bitcast.7, bf16[8,8,1024]{2,1,0:T(8,128)(2,1)} %bitcast.8, bf16[8,8,512]{2,1,0:T(8,128)(2,1)} %bitcast.9), custom_call_target="tpu_custom_call" | custom-call | tf_op jit(solution)/shard_map/pallas_call | solution.py:502
  54.4 1.6 %shard_map.69 = (bf16[4,8,512]{2,1,0:T(8,128)(2,1)}, bf16[8,8,1024]{2,1,0:T(8,128)(2,1)}) custom-call(bf16[4,8,512]{2,1,0:T(8,128)(2,1)} %get-tuple-element.6.rows_in, bf16[8,8,1024]{2,1,0:T(8,128)(2,1)} %get-tuple-element.7.nf_in), custom_call_target="tpu_custom_call" | custom-call | tf_op jit(solution)/shard_map/pallas_call | solution.py:512

commit v5 on v4

--- a/solution.py
+++ b/solution.py
@@ -322,11 +322,8 @@
         zall[z] = jnp.sum(sall[...], axis=(0, 1, 2))
         local = jnp.sum(sall[:, x])
 
-        def tell_z(k, _):
+        for k in (4, 3, 5, 2, 6, 1, 7):
             remote(zall.at[z], zall.at[z], z_s, z_r, i, lax.rem(z + k, NZ)).start()
-            return 0
-
-        lax.fori_loop(1, NZ, tell_z, 0)
         limit = CLIP_RMS * math.sqrt(ENTRIES)
 
         def clip_of(squares):
@@ -387,8 +384,11 @@
         nf_widths = [2 * width(q) for q in range(4)]
         res_widths = [BLK] * 4
         back(nf, nfr, nf_s, nf_r, nf_widths)
-        vm[...] = mm_tn(km[...], km[...]).astype(BF)
-        wm[...] = mm_tn(hm[...], hm[...]).astype(BF)
+        lo, hi = slice(0, HALF), slice(HALF, BLK)
+        for new, dst in ((km, vm), (hm, wm)):
+            dst[lo, :] = mm_tn(new[lo, lo], new[lo, :]).astype(BF)
+            dst[hi, lo] = mm_tn(new[lo, hi], new[lo, lo]).astype(BF)
+            dst[hi, hi] = mm_tn(new[:, hi], new[:, hi]).astype(BF)
         vm[...] = mm(vm[...], gbuf[...]).astype(BF)
         res[...] = mm(vm[...], wm[...]).reshape(N, ROWS, BLK).astype(BF)
 

time: 56.2 us -> 55.9 us (level)
  no operation moved by 1% of the time
where the time goes in v5:
time: 55.9 us; the launch traced here: 55.8 us
  Pallas kernels  55.1 us (99%)
  between operations  0.64 us (1%)
    pallas_call x1, Pallas kernels, body(): pl.pallas_call(kernel, out_shape=shapes, in_specs=[anywhere] * 5, out_spe...  53.5 us
    pallas_call x1, Pallas kernels, body(): pl.pallas_call(hand_on, out_shape=shapes, in_specs=[anywhere] * 2, out_sp...  1.6 us

profile of v5, /device:TPU:1, one launch (start us, length us, event | category | flops | bytes accessed | tf_op | source)
XLA Modules:
  0.0 55.8 jit_solution(18085547561107217554)
XLA Ops:
  0.6 53.5 %shard_map.68 = (bf16[4,8,512]{2,1,0:T(8,128)(2,1)}, bf16[8,8,1024]{2,1,0:T(8,128)(2,1)}) custom-call(s32[1,4]{1,0:T(1,128)} %t_hbm.1, bf16[4,512,512]{2,1,0:T(8,128)(2,1)} %bitcast.6, bf16[8,8,1024]{2,1,0:T(8,128)(2,1)} %bitcast.7, bf16[8,8,1024]{2,1,0:T(8,128)(2,1)} %bitcast.8, bf16[8,8,512]{2,1,0:T(8,128)(2,1)} %bitcast.9), custom_call_target="tpu_custom_call" | custom-call | tf_op jit(solution)/shard_map/pallas_call | solution.py:502
  54.2 1.6 %shard_map.69 = (bf16[4,8,512]{2,1,0:T(8,128)(2,1)}, bf16[8,8,1024]{2,1,0:T(8,128)(2,1)}) custom-call(bf16[4,8,512]{2,1,0:T(8,128)(2,1)} %get-tuple-element.6.rows_in, bf16[8,8,1024]{2,1,0:T(8,128)(2,1)} %get-tuple-element.7.nf_in), custom_call_target="tpu_custom_call" | custom-call | tf_op jit(solution)/shard_map/pallas_call | solution.py:512
